TPU v7x, 128 devices: a whole 4x4x4 slice. The times are simulated.
128 devices in a mesh: dp: 2 (over x_hi), fsdp: 16 (over y, z), tensor: 4 (over x_lo, core).
Axes of the slice: x: 4 (x_hi: 2, x_lo: 2; x = x_hi * 2 + x_lo), y: 4, z: 4, core: 2. Of those that a mesh axis runs over, the one named last changes fastest.
Arguments:
- x_in: bfloat16 [32, 512, 4608], P(('dp', 'fsdp'), None, 'tensor'), may hold values from -6 to 6
- lengths: int32 [32], P(('dp', 'fsdp')), may hold values from 128 to 512, as said below
- adapter_ids: int32 [32], P(('dp', 'fsdp')), may hold values from 0 to 15
- attn_grad: bfloat16 [32, 512, 4096], P(('dp', 'fsdp'), None, 'tensor'), may hold values from -6 to 6
- w_query: bfloat16 [4608, 4096], P('fsdp', 'tensor'), may hold values from -0.09375 to 0.09375
- w_key: bfloat16 [4608, 2048], P('fsdp', 'tensor'), may hold values from -0.09375 to 0.09375
- w_value: bfloat16 [4608, 2048], P('fsdp', 'tensor'), may hold values from -0.09375 to 0.09375
- query_down: bfloat16 [16, 16, 4608], replicated, may hold values from -0.09375 to 0.09375
- query_up: bfloat16 [16, 16, 4096], P(None, None, 'tensor'), may hold values from -1.5 to 1.5
- value_down: bfloat16 [16, 16, 4608], replicated, may hold values from -0.09375 to 0.09375
- value_up: bfloat16 [16, 16, 2048], P(None, None, 'tensor'), may hold values from -1.5 to 1.5
Outputs:
- grad_input: bfloat16 [32, 512, 4608], P(('dp', 'fsdp'), None, 'tensor')
- grad_query_down: float32 [16, 16, 4608], P(None, None, 'tensor')
- grad_query_up: float32 [16, 16, 4096], P(None, None, 'tensor')
- grad_value_down: float32 [16, 16, 4608], P(None, None, 'tensor')
- grad_value_up: float32 [16, 16, 2048], P(None, None, 'tensor')
Inputs may be any that keep to these rules, and one draw needn't show every extreme that they name: lengths[0] is 512.
All inputs are finite; a program needn't handle non-finite values.
Results may differ from a plain program's by a relative error of at most 0.012.
The roundings to bfloat16 on the way count: a program that leaves them out, or rounds other values in their place, can miss the bound.
Values may be sent and summed in bfloat16 or wider, within the bound.
A program may use at most 128 MiB of HBM per device.

v0:
```python
import math

import jax
import jax.numpy as jnp
from jax import lax
from jax.sharding import PartitionSpec as P

D = 4608
HEADS = 32
HD = 128


soft_cap = 50.0
adapter_scale = 2.0


def core_backward(
    input_rows,
    cotangent,
    length,
    down_q,
    query_up_weight,
    down_v,
    value_up_weight,
    frozen_query_weight,
    base_k,
    frozen_value_weight,
):
    count = input_rows.shape[0]
    score_scale = 1.0 / math.sqrt(D // HEADS)
    low_rank_query = lax.dot_general(
        input_rows, down_q, (((1,), (1,)), ((), ())), preferred_element_type=jnp.float32
    ).astype(jnp.bfloat16)
    low_rank_value = lax.dot_general(
        input_rows, down_v, (((1,), (1,)), ((), ())), preferred_element_type=jnp.float32
    ).astype(jnp.bfloat16)
    query_rows = (
        frozen_query_weight
        + adapter_scale
        * jnp.dot(low_rank_query, query_up_weight, preferred_element_type=jnp.float32)
    ).astype(jnp.bfloat16)
    keys = base_k.astype(jnp.bfloat16)
    value_rows = (
        frozen_value_weight
        + adapter_scale
        * jnp.dot(low_rank_value, value_up_weight, preferred_element_type=jnp.float32)
    ).astype(jnp.bfloat16)
    kv_count = keys.shape[1] // HD
    group_size = query_rows.shape[1] // keys.shape[1]
    query_heads = query_rows.reshape(count, kv_count, group_size, HD)
    key_heads = keys.reshape(count, kv_count, HD)
    value_heads = value_rows.reshape(count, kv_count, HD)
    raw = (
        jnp.einsum("ikgh,jkh->kgij", query_heads, key_heads, preferred_element_type=jnp.float32)
        * score_scale
    )
    capped = soft_cap * jnp.tanh(raw / soft_cap)
    positions = lax.iota(jnp.int32, count)
    allowed = (positions[None, :] <= positions[:, None]) & (positions[None, :] < length)
    weights = jnp.where(allowed, jnp.exp(capped), 0.0)
    probs = weights / jnp.sum(weights, axis=-1, keepdims=True)
    probs_b = probs.astype(jnp.bfloat16)
    row_used = positions < length
    cot = jnp.where(row_used[:, None], cotangent, jnp.zeros_like(cotangent))
    cot_heads = cot.reshape(count, kv_count, group_size, HD)
    dprob = jnp.einsum("ikgh,jkh->kgij", cot_heads, value_heads, preferred_element_type=jnp.float32)
    row_total = jnp.sum(probs * dprob, axis=-1, keepdims=True)
    dscore = (probs * (dprob - row_total) * (1.0 - (capped / soft_cap) ** 2) * score_scale).astype(
        jnp.bfloat16
    )
    query_gradient = (
        jnp.einsum("kgij,jkh->ikgh", dscore, key_heads, preferred_element_type=jnp.float32)
        .reshape(count, -1)
        .astype(jnp.bfloat16)
    )
    dkey = (
        jnp.einsum("kgij,ikgh->jkh", dscore, query_heads, preferred_element_type=jnp.float32)
        .reshape(count, -1)
        .astype(jnp.bfloat16)
    )
    value_gradient = (
        jnp.einsum("kgij,ikgh->jkh", probs_b, cot_heads, preferred_element_type=jnp.float32)
        .reshape(count, -1)
        .astype(jnp.bfloat16)
    )
    return (low_rank_query, low_rank_value, query_gradient, dkey, value_gradient)


def pick_adapter(chosen_row, table):
    return jnp.einsum("a,ard->rd", chosen_row, table, preferred_element_type=jnp.float32).astype(
        jnp.bfloat16
    )


def flipped_matrix_product(left, right):
    return lax.dot_general(
        left, right, (((1,), (1,)), ((), ())), preferred_element_type=jnp.float32
    )


def shards(
    x_in,
    lengths,
    adapter_ids,
    attn_grad,
    w_query,
    w_key,
    w_value,
    query_down,
    query_up,
    value_down,
    value_up,
):
    x_local = x_in[0]
    local_width = x_local.shape[1]
    length = lengths[0]
    x_whole = lax.all_gather(x_local, "tensor", axis=1, tiled=True)
    query_adapter_rows, rows_k, value_adapter_rows = (
        lax.all_gather(w_query, "fsdp", axis=0, tiled=True),
        lax.all_gather(w_key, "fsdp", axis=0, tiled=True),
        lax.all_gather(w_value, "fsdp", axis=0, tiled=True),
    )
    frozen_query_weight = jnp.dot(x_whole, query_adapter_rows, preferred_element_type=jnp.float32)
    base_k = jnp.dot(x_whole, rows_k, preferred_element_type=jnp.float32)
    frozen_value_weight = jnp.dot(x_whole, value_adapter_rows, preferred_element_type=jnp.float32)
    adapter_count = query_down.shape[0]
    chosen_row = (lax.iota(jnp.int32, adapter_count) == adapter_ids[0]).astype(jnp.bfloat16)
    down_q = pick_adapter(chosen_row, query_down)
    query_up_weight = pick_adapter(chosen_row, query_up)
    down_v = pick_adapter(chosen_row, value_down)
    value_up_weight = pick_adapter(chosen_row, value_up)
    low_rank_query, low_rank_value, query_gradient, dkey, value_gradient = core_backward(
        x_whole,
        attn_grad[0],
        length,
        down_q,
        query_up_weight,
        down_v,
        value_up_weight,
        frozen_query_weight,
        base_k,
        frozen_value_weight,
    )
    query_portion = adapter_scale * flipped_matrix_product(query_gradient, query_up_weight)
    value_portion = adapter_scale * flipped_matrix_product(value_gradient, value_up_weight)
    sum_q, sum_v = lax.psum((query_portion, value_portion), "tensor")
    low_rank_query_gradient = sum_q.astype(jnp.bfloat16)
    low_rank_value_gradient = sum_v.astype(jnp.bfloat16)
    partial_value = flipped_matrix_product(query_gradient, query_adapter_rows)
    partial_value = partial_value + flipped_matrix_product(dkey, rows_k)
    partial_value = partial_value + flipped_matrix_product(value_gradient, value_adapter_rows)
    summed = lax.psum_scatter(partial_value, "tensor", scatter_dimension=1, tiled=True)
    first_column = lax.axis_index("tensor") * local_width
    slice_q = lax.dynamic_slice_in_dim(down_q, first_column, local_width, 1)
    slice_v = lax.dynamic_slice_in_dim(down_v, first_column, local_width, 1)
    summed = summed + jnp.dot(low_rank_query_gradient, slice_q, preferred_element_type=jnp.float32)
    summed = summed + jnp.dot(low_rank_value_gradient, slice_v, preferred_element_type=jnp.float32)
    grad_input = summed.astype(jnp.bfloat16)[None]
    term_qa = jnp.dot(low_rank_query_gradient.T, x_local, preferred_element_type=jnp.float32)
    query_up_contribution = adapter_scale * jnp.dot(
        low_rank_query.T, query_gradient, preferred_element_type=jnp.float32
    )
    term_va = jnp.dot(low_rank_value_gradient.T, x_local, preferred_element_type=jnp.float32)
    value_up_contribution = adapter_scale * jnp.dot(
        low_rank_value.T, value_gradient, preferred_element_type=jnp.float32
    )
    owner_row = chosen_row.astype(jnp.float32)
    grad_qa, grad_qb, grad_va, grad_vb = lax.psum(
        (
            owner_row[:, None, None] * term_qa[None],
            owner_row[:, None, None] * query_up_contribution[None],
            owner_row[:, None, None] * term_va[None],
            owner_row[:, None, None] * value_up_contribution[None],
        ),
        ("dp", "fsdp"),
    )
    return (grad_input, grad_qa, grad_qb, grad_va, grad_vb)


def solution(mesh):
    placed = (
        P(("dp", "fsdp"), None, "tensor"),
        P(("dp", "fsdp")),
        P(("dp", "fsdp")),
        P(("dp", "fsdp"), None, "tensor"),
        P("fsdp", "tensor"),
        P("fsdp", "tensor"),
        P("fsdp", "tensor"),
        P(),
        P(None, None, "tensor"),
        P(),
        P(None, None, "tensor"),
    )
    return jax.shard_map(
        shards,
        mesh=mesh,
        in_specs=placed,
        out_specs=(
            P(("dp", "fsdp"), None, "tensor"),
            P(None, None, "tensor"),
            P(None, None, "tensor"),
            P(None, None, "tensor"),
            P(None, None, "tensor"),
        ),
        check_vma=False,
    )
```

profile of v0, /device:TPU:0, one launch (start us, length us, event | category | flops | bytes accessed | tf_op | source)
XLA Modules:
  0.0 804.3 jit_solution(9568788227685811203)
XLA Ops:
  11.3 2.7 fusion.25
  14.1 4.4 fusion.23
  20.6 1.5 fusion.53
  22.1 40.4 %all-gather.12.cloned.1.call-done = bf16[1,512,4608]{2,1,0:T(8,128)(2,1)} async-done(((bf16[1,512,1152]{2,1,0:T(8,128)(2,1)}), bf16[1,512,4608]{2,1,0:T(8,128)(2,1)}) %all-gather.12.cloned.1.call-update) | async-done | bytes 4718608 | tf_op jit(solution)/shard_map/all_gather | solution.py:117
  62.5 3.7 fusion.45
  66.1 3.7 fusion.48
  69.8 50.5 %all-gather.10.cloned.1.call-done = bf16[4608,512]{1,0:T(8,128)(2,1)} async-done(((bf16[288,512]{1,0:T(8,128)(2,1)}), bf16[4608,512]{1,0:T(8,128)(2,1)}) %all-gather.10.cloned.1.call-update) | async-done | bytes 4718608 | tf_op jit(solution)/shard_map/all_gather | solution.py:121
  120.3 5.9 fusion.8
  126.6 4.6 fusion.52
  131.2 45.0 %all-gather.6.cloned.1.call-done = bf16[4608,512]{1,0:T(8,128)(2,1)} async-done(((bf16[288,512]{1,0:T(8,128)(2,1)}), bf16[4608,512]{1,0:T(8,128)(2,1)}) %all-gather.6.cloned.1.call-update) | async-done | bytes 4718608 | tf_op jit(solution)/shard_map/all_gather | solution.py:120
  176.2 6.4 fusion.37
  182.6 70.9 %all-gather.8.cloned.1.call-done = bf16[4608,1024]{1,0:T(8,128)(2,1)} async-done(((bf16[288,1024]{1,0:T(8,128)(2,1)}), bf16[4608,1024]{1,0:T(8,128)(2,1)}) %all-gather.8.cloned.1.call-update) | async-done | bytes 9437200 | tf_op jit(solution)/shard_map/all_gather | solution.py:119
  253.6 9.0 %fusion.12 = f32[512,1024]{1,0:T(8,128)S(1)} fusion(bf16[4608,1024]{1,0:T(8,128)(2,1)} %all-gather.8.cloned.1.call-done, bf16[1,512,4608]{2,1,0:T(8,128)(2,1)} %all-gather.12.cloned.1.call-done), kind=kOutput, calls=%fused_computation.18 | convolution fusion | flops 4831838208 | bytes 16252928 | tf_op jit(solution)/shard_map/dot_general | solution.py:123
  263.0 1.3 copy.47
  264.3 4.0 fusion.5
  268.3 3.3 copy-done.11
  271.7 3.1 fusion.33
  274.8 18.3 %fusion.36 = bf16[4,128,512]{2,1,0:T(8,128)(2,1)S(1)} fusion(bf16[512,4,2,128]{0,3,2,1:T(8,128)(2,1)S(1)} %bitcast.203, f32[4,512,512,2]{2,1,3,0:T(8,128)} %fusion.52, f32[4,512,512,2]{2,1,3,0:T(8,128)} %copy-done.11, f32[4,2,512]{2,1,0:T(2,128)S(1)} %get-tuple-element.13, pred[512,512]{0,1:T(8,128)(4,1)S(1)} %fusion.51), kind=kOutput, calls=%fused_computation.42 | convolution fusion | flops 570692096 | bytes 18628608 | tf_op jit(solution)/shard_map/kgij,ikgh->jkh/dot_general | solution.py:77
  293.1 14.3 %fusion.27 = bf16[4,128,2,512]{3,1,2,0:T(8,128)(2,1)S(1)} fusion(bf16[512,4,128,1]{0,2,3,1:T(8,128)(2,1)S(1)} %bitcast.210, f32[4,512,512,2]{2,1,3,0:T(8,128)} %fusion.52, f32[4,512,512,2]{2,1,3,0:T(8,128)} %copy-done.11, f32[4,2,512]{2,1,0:T(2,128)S(1)} %get-tuple-element.13, pred[512,512]{0,1:T(8,128)(4,1)S(1)} %fusion.51), kind=kOutput, calls=%fused_computation.36 | convolution fusion | flops 570954240 | bytes 18628608 | tf_op jit(solution)/shard_map/kgij,jkh->ikgh/dot_general | solution.py:72
  307.4 11.3 %fusion.90 = f32[512,4608]{1,0:T(8,128)} fusion(bf16[512,1024]{0,1:T(8,128)(2,1)S(1)} %bitcast.198, bf16[4608,1024]{1,0:T(8,128)(2,1)} %all-gather.8.cloned.1.call-done), kind=kOutput, calls=%fused_computation.102 | convolution fusion | flops 4831838208 | bytes 19922944 | tf_op jit(solution)/shard_map/dot_general | solution.py:96
  318.7 4.6 fusion.91
  323.3 9.3 %add_add_fusion = f32[512,4608]{1,0:T(8,128)} fusion(f32[512,4608]{1,0:T(8,128)} %fusion.90, f32[512,4608]{1,0:T(8,128)S(1)} %fusion.91, bf16[512,512]{0,1:T(8,128)(2,1)S(1)} %bitcast.193, bf16[4608,512]{1,0:T(8,128)(2,1)} %all-gather.10.cloned.1.call-done), kind=kOutput, calls=%fused_computation.1 | convolution fusion | flops 2420637696 | bytes 33554432 | tf_op jit(solution)/shard_map/dot_general | solution.py:96
  333.1 12.5 %all-reduce.1 = (bf16[512,16]{0,1:T(8,128)(2,1)S(1)}, bf16[512,16]{0,1:T(8,128)(2,1)S(1)}) all-reduce(f32[512,16]{0,1:T(8,128)S(1)} %convolution_multiply_fusion.2, f32[512,16]{0,1:T(8,128)S(1)} %convolution_multiply_fusion.3), channel_id=1, replica_groups=mesh['dp'=2,'fsdp'=16,'tensor'=4] {'tensor'}, use_global_device_ids=true, to_apply=%region_3.4 | all-reduce | flops 16384 | bytes 98304 | tf_op jit(solution)/shard_map/psum | solution.py:146
  348.8 1.6 broadcast_multiply_fusion
  350.5 69.5 %reduce-scatter.2.cloned.1.call-done = f32[512,1152]{1,0:T(8,128)} async-done(((f32[512,4608]{1,0:T(8,128)}), f32[512,1152]{1,0:T(8,128)}) %reduce-scatter.2.cloned.1.call-update) | async-done | bytes 2359312 | tf_op jit(solution)/shard_map/reduce_scatter | solution.py:152
  420.0 2.2 convolution_add_fusion.1
  422.2 1.5 fusion.22
  423.7 364.9 %all-reduce.4.cloned.1.call-done = (f32[16,16,1152]{2,1,0:T(8,128)}, f32[16,16,1024]{2,1,0:T(8,128)}, f32[16,16,1152]{2,1,0:T(8,128)}, f32[16,16,512]{2,1,0:T(8,128)}) async-done(((f32[16,16,1152]{2,1,0:T(8,128)}, f32[16,16,1024]{2,1,0:T(8,128)}, f32[16,16,1152]{2,1,0:T(8,128)}, f32[16,16,512]{2,1,0:T(8,128)}), (f32[16,16,1152]{2,1,0:T(8,128)}, f32[16,16,1024]{2,1,0:T(8,128)}, f32[16,16,1152]{2,1,0:T(8,128)}, ...) | async-done | bytes 3932176 | tf_op jit(solution)/shard_map/psum | solution.py:168
  788.6 2.4 copy.72
  790.9 2.3 copy.73
  793.3 2.4 copy.74
  795.6 1.9 copy.75
  (52 shorter events, 9.4 us)
Async XLA Ops:
  7.2 4.2 copy-start
  7.2 11.3 %copy-start.3 = (bf16[1,512,1024]{2,1,0:T(8,128)(2,1)S(1)}, bf16[1,512,1024]{2,1,0:T(8,128)(2,1)}, u32[]{:S(2)}) copy-start(bf16[1,512,1024]{2,1,0:T(8,128)(2,1)} %param.14) | copy-start | bytes 3145732
  7.2 55.3 %all-gather.12.cloned.1.call-start = ((), (), s32[]{:S(2)}) async-start(), calls=%async_computation.5 | async-start | bytes 5898240 | tf_op jit(solution)/shard_map/all_gather | solution.py:117
  7.9 112.4 %all-gather.10.cloned.1.call-start = ((), (), s32[]{:S(2)}) async-start(), calls=%async_computation.3 | async-start | bytes 5013504 | tf_op jit(solution)/shard_map/all_gather | solution.py:121
  8.7 167.5 %all-gather.6.cloned.1.call-start = ((), (), s32[]{:S(2)}) async-start(), calls=%async_computation.1 | async-start | bytes 5013504 | tf_op jit(solution)/shard_map/all_gather | solution.py:120
  9.4 244.1 %all-gather.8.cloned.1.call-start = ((), (), s32[]{:S(2)}) async-start(), calls=%async_computation.2 | async-start | bytes 10027008 | tf_op jit(solution)/shard_map/all_gather | solution.py:119
  10.0 410.0 %reduce-scatter.2.cloned.1.call-start = ((), (), s32[]{:S(2)}) async-start(), calls=%async_computation.4 | async-start | bytes 11796480 | tf_op jit(solution)/shard_map/reduce_scatter | solution.py:152
  14.0 106.2 %copy-start.5 = (bf16[1,16,4608]{2,1,0:T(8,128)(2,1)}, bf16[1,16,4608]{2,1,0:T(8,128)(2,1)S(1)}, u32[]{:S(2)}) copy-start(bf16[1,16,4608]{2,1,0:T(8,128)(2,1)S(1)} %copy.65) | copy-start | bytes 442372
  182.6 81.7 %copy-start.9 = (bf16[512,512]{0,1:T(8,128)(2,1)}, bf16[512,512]{0,1:T(8,128)(2,1)S(1)}, u32[]{:S(2)}) copy-start(bf16[512,512]{0,1:T(8,128)(2,1)S(1)} %fusion.37) | copy-start | bytes 1572868
  268.3 3.3 copy-start.11
  271.7 3.1 copy-start.4
  274.8 18.3 %copy-start.10 = (bf16[512,512]{0,1:T(8,128)(2,1)S(1)}, bf16[512,512]{0,1:T(8,128)(2,1)}, u32[]{:S(2)}) copy-start(bf16[512,512]{0,1:T(8,128)(2,1)} %copy-done.9) | copy-start | bytes 1572868
  332.5 15.7 %copy-start.2 = (bf16[1,512,1152]{2,1,0:T(8,128)(2,1)S(1)}, bf16[1,512,1152]{2,1,0:T(8,128)(2,1)}, u32[]{:S(2)}) copy-start(bf16[1,512,1152]{2,1,0:T(8,128)(2,1)} %param.11) | copy-start | bytes 3538948
  332.6 456.0 %all-reduce.4.cloned.1.call-start = ((), (), s32[]{:S(2)}) async-start(), calls=%async_computation.6 | async-start | bytes 7864320 | tf_op jit(solution)/shard_map/psum | solution.py:168
  345.6 4.8 copy-start.6
  345.6 4.8 copy-start.8
  350.4 71.7 %copy-start.7 = (bf16[512,16]{0,1:T(8,128)(2,1)S(1)}, bf16[512,16]{0,1:T(8,128)(2,1)}, u32[]{:S(2)}) copy-start(bf16[512,16]{0,1:T(8,128)(2,1)} %copy-done.6) | copy-start | bytes 49156
  350.5 447.0 %copy-start.1 = (bf16[16,16,4608]{2,1,0:T(8,128)(2,1)S(1)}, bf16[16,16,4608]{2,1,0:T(8,128)(2,1)}, u32[]{:S(2)}) copy-start(bf16[16,16,4608]{2,1,0:T(8,128)(2,1)} %param.18) | copy-start | bytes 7077892
Sparse Core Ops, SparseCore 0:
  9.7 52.7 all-gather.11
  64.6 55.5 all-gather.9
  122.5 53.6 all-gather.5
  178.3 75.2 all-gather.7
  332.7 87.2 reduce-scatter.1
  423.2 365.3 all-reduce.3
where the time goes:
time: 805 us; the launch traced here: 804 us
  waiting for transfers between devices  644 us (80%)
  matrix products  114 us (14%)
  between operations  15.6 us (2%)
  local copies, waits for them, and re-layouts  14.4 us (2%)
  blocking collectives  12.5 us (2%)
    psum x1, waiting for transfers between devices, shards(): lax.psum((owner_row[:, None, None] * term_qa[None], owner_row[:, None, No...  365 us
    all_gather x1, waiting for transfers between devices, shards(): lax.all_gather(w_query, 'fsdp', axis=0, tiled=True)  70.9 us
    reduce_scatter x1, waiting for transfers between devices, shards(): lax.psum_scatter(partial_value, 'tensor', scatter_dimension=1, tiled=True)  69.5 us
    all_gather x1, waiting for transfers between devices, shards(): lax.all_gather(w_value, 'fsdp', axis=0, tiled=True)  50.5 us
    all_gather x1, waiting for transfers between devices, shards(): lax.all_gather(w_key, 'fsdp', axis=0, tiled=True)  45 us
    all_gather x1, waiting for transfers between devices, shards(): x_whole = lax.all_gather(x_local, 'tensor', axis=1, tiled=True)  40.4 us
    dot_general x5, matrix products, flipped_matrix_product(): lax.dot_general(left, right, (((1,), (1,)), ((), ())), preferred_element_...  25.6 us
    dot_general x1, matrix products, core_backward(): jnp.einsum('kgij,ikgh->jkh', dscore, query_heads, preferred_element_type=...  18.3 us
  transfers between devices with their start and end apart: 6, of which 6 were waited for; matrix products, arithmetic and copies ran while one was open for 6% of the time, Pallas kernels for 0%

commit v1 on v0

--- a/solution.py
+++ b/solution.py
@@ -115,11 +115,14 @@
     local_width = x_local.shape[1]
     length = lengths[0]
     x_whole = lax.all_gather(x_local, "tensor", axis=1, tiled=True)
-    query_adapter_rows, rows_k, value_adapter_rows = (
-        lax.all_gather(w_query, "fsdp", axis=0, tiled=True),
-        lax.all_gather(w_key, "fsdp", axis=0, tiled=True),
-        lax.all_gather(w_value, "fsdp", axis=0, tiled=True),
-    )
+    all_ids = lax.all_gather(adapter_ids, ("dp", "fsdp"), axis=0, tiled=True)
+    w_rows = lax.all_gather(
+        jnp.concatenate([w_query, w_key, w_value], axis=1), "fsdp", axis=0, tiled=True
+    )
+    q_width, kv_width = w_query.shape[1], w_key.shape[1]
+    query_adapter_rows = w_rows[:, :q_width]
+    rows_k = w_rows[:, q_width : q_width + kv_width]
+    value_adapter_rows = w_rows[:, q_width + kv_width :]
     frozen_query_weight = jnp.dot(x_whole, query_adapter_rows, preferred_element_type=jnp.float32)
     base_k = jnp.dot(x_whole, rows_k, preferred_element_type=jnp.float32)
     frozen_value_weight = jnp.dot(x_whole, value_adapter_rows, preferred_element_type=jnp.float32)
@@ -164,16 +167,17 @@
     value_up_contribution = adapter_scale * jnp.dot(
         low_rank_value.T, value_gradient, preferred_element_type=jnp.float32
     )
-    owner_row = chosen_row.astype(jnp.float32)
-    grad_qa, grad_qb, grad_va, grad_vb = lax.psum(
-        (
-            owner_row[:, None, None] * term_qa[None],
-            owner_row[:, None, None] * query_up_contribution[None],
-            owner_row[:, None, None] * term_va[None],
-            owner_row[:, None, None] * value_up_contribution[None],
-        ),
-        ("dp", "fsdp"),
-    )
+    terms = jnp.concatenate(
+        [term_qa, query_up_contribution, term_va, value_up_contribution], axis=1
+    ).astype(jnp.bfloat16)
+    all_terms = lax.all_gather(terms, ("dp", "fsdp"), axis=0)
+    owners = (all_ids[:, None] == lax.iota(jnp.int32, adapter_count)[None, :]).astype(jnp.bfloat16)
+    tables = jnp.einsum("sa,srd->ard", owners, all_terms, preferred_element_type=jnp.float32)
+    qd, qu = term_qa.shape[1], query_up_contribution.shape[1]
+    grad_qa = tables[:, :, :qd]
+    grad_qb = tables[:, :, qd : qd + qu]
+    grad_va = tables[:, :, qd + qu : 2 * qd + qu]
+    grad_vb = tables[:, :, 2 * qd + qu :]
     return (grad_input, grad_qa, grad_qb, grad_va, grad_vb)
 
 

time: 805 us -> 436 us (0.54)
  waiting for transfers between devices: 644 us -> 249 us
  blocking collectives: 12.5 us -> 31.3 us
    psum x1 -> x0, waiting for transfers between devices: 365 us -> none  [shards(): lax.psum((owner_row[:, None, None] * term_qa[None], owner_row[:, None, No...]
    all_gather x3 -> x2, waiting for transfers between devices: 166 us -> 130 us  [the longest x1 117 us: shards(): lax.all_gather(jnp.concatenate([w_query, w_key, w_value], axis=1), 'fsdp'...]
    unnamed x0 -> x1, blocking collectives: none -> 19.3 us
    reduce_scatter x1, waiting for transfers between devices: 69.5 us -> 78.5 us  [shards(): lax.psum_scatter(partial_value, 'tensor', scatter_dimension=1, tiled=True)]
  transfers between devices with their start and end apart: 6 -> 4, of which waited for: 6 -> 4; matrix products, arithmetic and copies ran while one was open for 6% -> 18% of each run, Pallas kernels for 0% -> 0%
where the time goes in v1:
time: 436 us; the launch traced here: 430 us
  waiting for transfers between devices  249 us (57%)
  matrix products  122 us (28%)
  blocking collectives  31.3 us (7%)
  between operations  15.6 us (4%)
  local copies, waits for them, and re-layouts  9.01 us (2%)
    all_gather x1, waiting for transfers between devices, shards(): lax.all_gather(jnp.concatenate([w_query, w_key, w_value], axis=1), 'fsdp'...  117 us
    reduce_scatter x1, waiting for transfers between devices, shards(): lax.psum_scatter(partial_value, 'tensor', scatter_dimension=1, tiled=True)  78.5 us
    all_gather x1, waiting for transfers between devices, shards(): x_whole = lax.all_gather(x_local, 'tensor', axis=1, tiled=True)  39.5 us
    dot_general x5, matrix products, flipped_matrix_product(): lax.dot_general(left, right, (((1,), (1,)), ((), ())), preferred_element_...  30.6 us
    unnamed x1, blocking collectives  19.3 us
    dot_general x1, matrix products, core_backward(): jnp.einsum('kgij,ikgh->jkh', dscore, query_heads, preferred_element_type=...  15.2 us
    dot_general x1, matrix products, core_backward(): jnp.einsum('kgij,jkh->ikgh', dscore, key_heads, preferred_element_type=jn...  14.7 us
    all_gather x1, waiting for transfers between devices, shards(): all_terms = lax.all_gather(terms, ('dp', 'fsdp'), axis=0)  12.7 us
  transfers between devices with their start and end apart: 4, of which 4 were waited for; matrix products, arithmetic and copies ran while one was open for 18% of the time, Pallas kernels for 0%

profile of v1, /device:TPU:0, one launch (start us, length us, event | category | flops | bytes accessed | tf_op | source)
XLA Modules:
  0.0 430.1 jit_solution(13498650649095093086)
XLA Ops:
  8.0 2.6 pad_maximum_fusion
  12.0 2.7 fusion.38
  14.7 4.4 %fusion.36 = bf16[1,16,4608]{2,0,1:T(2,128)(2,1)S(1)} fusion(bf16[16,16,4608]{2,1,0:T(8,128)(2,1)} %param.20, s32[]{:T(128)} %bitcast.208), kind=kOutput, calls=%fused_computation.42 | convolution fusion | flops 2359312 | bytes 2506756 | tf_op jit(solution)/shard_map/a,ard->rd/dot_general | solution.py:90
  20.1 1.3 fusion.86
  21.5 1.5 fusion.82
  23.0 39.5 %all-gather.9.cloned.1.call-done = bf16[1,512,4608]{2,1,0:T(8,128)(2,1)} async-done(((bf16[1,512,1152]{2,1,0:T(8,128)(2,1)}), bf16[1,512,4608]{2,1,0:T(8,128)(2,1)}) %all-gather.9.cloned.1.call-update) | async-done | bytes 4718608 | tf_op jit(solution)/shard_map/all_gather | solution.py:117
  62.5 3.6 fusion.72
  66.1 1.8 fusion.90
  67.9 3.7 fusion.75
  71.6 117.3 %all-gather.5.cloned.1.call-done = bf16[4608,2048]{1,0:T(8,128)(2,1)} async-done(((bf16[288,2048]{1,0:T(8,128)(2,1)}), bf16[4608,2048]{1,0:T(8,128)(2,1)}) %all-gather.5.cloned.1.call-update) | async-done | bytes 18874384 | tf_op jit(solution)/shard_map/all_gather | solution.py:119
  188.9 6.6 %fusion.62 = bf16[512,512]{1,0:T(8,128)(2,1)S(1)} fusion(bf16[1,512,4608]{2,1,0:T(8,128)(2,1)} %all-gather.9.cloned.1.call-done, bf16[4608,2048]{1,0:T(8,128)(2,1)} %all-gather.5.cloned.1.call-done), kind=kOutput, calls=%fused_computation.60 | convolution fusion | flops 2416181248 | bytes 9961472 | tf_op jit(solution)/shard_map/dot_general | solution.py:127
  195.5 9.9 %fusion.42 = bf16[512,1024]{0,1:T(8,128)(2,1)S(1)} fusion(f32[512,1024]{0,1:T(8,128)S(1)} %copy-done.3, bf16[1,512,4608]{2,1,0:T(8,128)(2,1)} %all-gather.9.cloned.1.call-done, bf16[4608,2048]{1,0:T(8,128)(2,1)} %all-gather.5.cloned.1.call-done), kind=kOutput, calls=%fused_computation.51 | convolution fusion | flops 4833411072 | bytes 17301504 | tf_op jit(solution)/shard_map/dot_general | solution.py:126
  205.5 2.9 fusion.11
  208.4 3.6 fusion.58
  213.8 4.6 %fusion.52 = f32[512,512]{0,1:T(8,128)S(1)} fusion(bf16[1,512,4608]{2,1,0:T(8,128)(2,1)S(1)} %bitcast.211, bf16[4608,2048]{1,0:T(8,128)(2,1)} %all-gather.5.cloned.1.call-done), kind=kOutput, calls=%fused_computation.55 | convolution fusion | flops 2415919104 | bytes 10485760 | tf_op jit(solution)/shard_map/dot_general | solution.py:128
  218.7 4.6 %fusion.81 = f32[4,512,512,2]{2,1,3,0:T(8,128)} fusion(bf16[512,4,128,1]{0,2,3,1:T(8,128)(2,1)S(1)} %bitcast.220, bf16[512,4,2,128]{0,3,2,1:T(8,128)(2,1)S(1)} %bitcast.216, pred[512]{0:T(512)(128)(4,1)S(1)} %iota_compare_fusion.2), kind=kOutput, calls=%fused_computation.78 | convolution fusion | flops 537395200 | bytes 9961984 | tf_op jit(solution)/shard_map/ikgh,jkh->kgij/dot_general | solution.py:66
  223.3 14.7 %fusion.47 = bf16[4,128,2,512]{3,1,2,0:T(8,128)(2,1)S(1)} fusion(bf16[512,4,128,1]{0,2,3,1:T(8,128)(2,1)} %bitcast.229, f32[4,512,512,2]{2,1,3,0:T(8,128)} %fusion.81, f32[4,512,512,2]{2,1,3,0:T(8,128)} %copy-done.16, f32[4,2,512]{2,1,0:T(2,128)S(1)} %copy-done.18, pred[512,512]{0,1:T(8,128)(4,1)} %copy-done.6), kind=kOutput, calls=%fused_computation.52 | convolution fusion | flops 570954240 | bytes 18628608 | tf_op jit(solution)/shard_map/kgij,jkh->ikgh/dot_general | solution.py:72
  238.6 12.0 %all-reduce.1 = (bf16[512,16]{0,1:T(8,128)(2,1)S(1)}, bf16[512,16]{0,1:T(8,128)(2,1)S(1)}) all-reduce(f32[512,16]{0,1:T(8,128)S(1)} %convolution_multiply_fusion.2, f32[512,16]{0,1:T(8,128)S(1)} %copy-done.7), channel_id=1, replica_groups=mesh['dp'=2,'fsdp'=16,'tensor'=4] {'tensor'}, use_global_device_ids=true, to_apply=%region_3.4 | all-reduce | flops 16384 | bytes 98304 | tf_op jit(solution)/shard_map/psum | solution.py:149
  252.2 15.2 %fusion.61 = bf16[4,128,512]{2,1,0:T(8,128)(2,1)S(1)} fusion(bf16[512,4,2,128]{0,3,2,1:T(8,128)(2,1)} %bitcast.227, f32[4,512,512,2]{2,1,3,0:T(8,128)} %fusion.81, f32[4,512,512,2]{2,1,3,0:T(8,128)} %copy-done.16, f32[4,2,512]{2,1,0:T(2,128)} %copy-done.17, pred[512,512]{0,1:T(8,128)(4,1)} %copy-done.6), kind=kOutput, calls=%fused_computation.59 | convolution fusion | flops 570692096 | bytes 18628608 | tf_op jit(solution)/shard_map/kgij,ikgh->jkh/dot_general | solution.py:77
  267.4 7.5 %fusion.23 = f32[512,4608]{1,0:T(8,128)} fusion(bf16[512,512]{0,1:T(8,128)(2,1)S(1)} %bitcast.214, bf16[4608,2048]{1,0:T(8,128)(2,1)} %all-gather.5.cloned.1.call-done), kind=kOutput, calls=%fused_computation.27 | convolution fusion | flops 2415919104 | bytes 14680064 | tf_op jit(solution)/shard_map/dot_general | solution.py:96
  274.9 7.5 %fusion.26 = f32[512,4608]{1,0:T(8,128)} fusion(bf16[512,512]{0,1:T(8,128)(2,1)S(1)} %bitcast.225, bf16[4608,2048]{1,0:T(8,128)(2,1)} %all-gather.5.cloned.1.call-done), kind=kOutput, calls=%fused_computation.30 | convolution fusion | flops 2415919104 | bytes 14680064 | tf_op jit(solution)/shard_map/dot_general | solution.py:96
  282.4 14.5 %add_add_fusion = f32[512,4608]{1,0:T(8,128)} fusion(f32[512,4608]{1,0:T(8,128)} %fusion.23, f32[512,4608]{1,0:T(8,128)} %fusion.26, bf16[512,1024]{0,1:T(8,128)(2,1)S(1)} %bitcast.219, bf16[4608,2048]{1,0:T(8,128)(2,1)} %all-gather.5.cloned.1.call-done), kind=kOutput, calls=%fused_computation.1 | convolution fusion | flops 4836556800 | bytes 38797312 | tf_op jit(solution)/shard_map/dot_general | solution.py:96
  298.9 19.3 %all-reduce = s32[32]{0:T(128)S(1)} all-reduce(s32[32]{0:T(128)S(1)} %dynamic-update-slice), channel_id=1, replica_groups=mesh['dp'=2,'fsdp'=16,'tensor'=4] {'dp','fsdp'}, use_global_device_ids=true, to_apply=%add | all-reduce | flops 32 | bytes 256
  318.3 12.7 %all-gather.7.cloned.1.call-done = bf16[32,16,3840]{2,1,0:T(8,128)(2,1)} async-done(((bf16[1,16,3840]{2,1,0:T(8,128)(2,1)}), bf16[32,16,3840]{2,1,0:T(8,128)(2,1)}) %all-gather.7.cloned.1.call-update) | async-done | bytes 3932176 | tf_op jit(solution)/shard_map/all_gather | solution.py:173
  330.9 4.4 %fusion.29 = f32[16,16,3840]{2,0,1:T(8,128)S(1)} fusion(bf16[32,16,3840]{2,1,0:T(8,128)(2,1)} %all-gather.7.cloned.1.call-done, s32[32]{0:T(128)S(1)} %all-reduce), kind=kOutput, calls=%fused_computation.33 | convolution fusion | flops 62915072 | bytes 7864448 | tf_op jit(solution)/shard_map/sa,srd->ard/dot_general | solution.py:175
  335.5 1.1 copy.43
  336.8 1.4 copy.42
  338.2 1.6 copy.41
  339.8 1.4 copy.40
  341.1 78.5 %reduce-scatter.2.cloned.1.call-done = f32[512,1152]{1,0:T(8,128)} async-done(((f32[512,4608]{1,0:T(8,128)}), f32[512,1152]{1,0:T(8,128)}) %reduce-scatter.2.cloned.1.call-update) | async-done | bytes 2359312 | tf_op jit(solution)/shard_map/reduce_scatter | solution.py:155
  419.6 2.2 convolution_add_fusion.1
  421.8 1.5 fusion.35
  (70 shorter events, 8.4 us)
Async XLA Ops:
  7.2 4.8 %copy-start = (bf16[16,16,4608]{2,1,0:T(8,128)(2,1)S(1)}, bf16[16,16,4608]{2,1,0:T(8,128)(2,1)}, u32[]{:S(2)}) copy-start(bf16[16,16,4608]{2,1,0:T(8,128)(2,1)} %param.18) | copy-start | bytes 7077892
  7.2 11.9 %copy-start.4 = (bf16[1,512,1024]{2,1,0:T(8,128)(2,1)S(1)}, bf16[1,512,1024]{2,1,0:T(8,128)(2,1)}, u32[]{:S(2)}) copy-start(bf16[1,512,1024]{2,1,0:T(8,128)(2,1)} %param.14) | copy-start | bytes 3145732
  7.2 55.3 %all-gather.9.cloned.1.call-start = ((), (), s32[]{:S(2)}) async-start(), calls=%async_computation.4 | async-start | bytes 5898240 | tf_op jit(solution)/shard_map/all_gather | solution.py:117
  7.9 181.0 %all-gather.5.cloned.1.call-start = ((), (), s32[]{:S(2)}) async-start(), calls=%async_computation.1 | async-start | bytes 20054016 | tf_op jit(solution)/shard_map/all_gather | solution.py:119
  10.6 320.3 %all-gather.7.cloned.1.call-start = ((), (), s32[]{:S(2)}) async-start(), calls=%async_computation.3 | async-start | bytes 4055040 | tf_op jit(solution)/shard_map/all_gather | solution.py:173
  14.7 56.9 %copy-start.5 = (bf16[1,16,4608]{2,1,0:T(8,128)(2,1)}, bf16[1,16,4608]{2,1,0:T(8,128)(2,1)S(1)}, u32[]{:S(2)}) copy-start(bf16[1,16,4608]{2,1,0:T(8,128)(2,1)S(1)} %copy.87) | copy-start | bytes 442372
  20.1 188.3 %copy-start.6 = (pred[512,512]{0,1:T(8,128)(4,1)}, pred[512,512]{0,1:T(8,128)(4,1)S(1)}, u32[]{:S(2)}) copy-start(pred[512,512]{0,1:T(8,128)(4,1)S(1)} %fusion.80) | copy-start | bytes 786436
  188.9 6.6 %copy-start.3 = (f32[512,1024]{0,1:T(8,128)S(1)}, f32[512,1024]{0,1:T(8,128)}, u32[]{:S(2)}) copy-start(f32[512,1024]{0,1:T(8,128)} %fusion.90) | copy-start | bytes 6291460
  195.5 10.0 %copy-start.14 = (bf16[512,512]{1,0:T(8,128)(2,1)}, bf16[512,512]{1,0:T(8,128)(2,1)S(1)}, u32[]{:S(2)}) copy-start(bf16[512,512]{1,0:T(8,128)(2,1)S(1)} %fusion.62) | copy-start | bytes 1572868
  205.5 6.6 %copy-start.13 = (bf16[512,1024]{0,1:T(8,128)(2,1)}, bf16[512,1024]{0,1:T(8,128)(2,1)S(1)}, u32[]{:S(2)}) copy-start(bf16[512,1024]{0,1:T(8,128)(2,1)S(1)} %fusion.42) | copy-start | bytes 3145732
  205.5 8.3 %slice-start = ((s8[4718592]{0:T(1024)(128)(4,1)}), s8[4194304]{0:T(1024)(128)(4,1)S(1)}, s32[]{:S(2)}) async-start(s8[4718592]{0:T(1024)(128)(4,1)} %bitcast.210), calls=%async_computation.5 | async-start | bytes 8388608
  208.4 3.7 copy-start.16
  208.4 3.7 copy-start.17
  208.4 5.4 %slice-start.1 = ((s8[4718592]{0:T(1024)(128)(4,1)}), s8[524288]{0:T(1024)(128)(4,1)S(1)}, s32[]{:S(2)}) async-start(s8[4718592]{0:T(1024)(128)(4,1)} %bitcast.210), calls=%async_computation.6 | async-start | bytes 1048576
  218.7 4.6 %copy-start.18 = (f32[4,2,512]{2,1,0:T(2,128)S(1)}, f32[4,2,512]{2,1,0:T(2,128)}, u32[]{:S(2)}) copy-start(f32[4,2,512]{2,1,0:T(2,128)} %copy-done.17) | copy-start | bytes 49156
  223.3 15.3 %copy-start.7 = (f32[512,16]{0,1:T(8,128)S(1)}, f32[512,16]{0,1:T(8,128)}, u32[]{:S(2)}) copy-start(f32[512,16]{0,1:T(8,128)} %convolution_multiply_fusion.3) | copy-start | bytes 98308
  223.3 27.3 %copy-start.2 = (bf16[1,512,1152]{2,1,0:T(8,128)(2,1)S(1)}, bf16[1,512,1152]{2,1,0:T(8,128)(2,1)}, u32[]{:S(2)}) copy-start(bf16[1,512,1152]{2,1,0:T(8,128)(2,1)} %param.11) | copy-start | bytes 3538948
  223.3 28.2 %copy-start.12 = (bf16[1,16,512]{2,1,0:T(8,128)(2,1)S(1)}, bf16[1,16,512]{2,1,0:T(8,128)(2,1)}, u32[]{:S(2)}) copy-start(bf16[1,16,512]{2,1,0:T(8,128)(2,1)} %fusion.79) | copy-start | bytes 49156
  250.6 0.6 copy-start.10
  250.6 16.8 %copy-start.8 = (bf16[512,16]{0,1:T(8,128)(2,1)}, bf16[512,16]{0,1:T(8,128)(2,1)S(1)}, u32[]{:S(2)}) copy-start(bf16[512,16]{0,1:T(8,128)(2,1)S(1)} %get-tuple-element.16) | copy-start | bytes 49156
  252.1 167.5 %reduce-scatter.2.cloned.1.call-start = ((), (), s32[]{:S(2)}) async-start(), calls=%async_computation.2 | async-start | bytes 11796480 | tf_op jit(solution)/shard_map/reduce_scatter | solution.py:155
  296.9 0.7 copy-start.15
  335.3 84.3 %copy-start.11 = (bf16[512,16]{0,1:T(8,128)(2,1)S(1)}, bf16[512,16]{0,1:T(8,128)(2,1)}, u32[]{:S(2)}) copy-start(bf16[512,16]{0,1:T(8,128)(2,1)} %copy-done.10) | copy-start | bytes 49156
  336.6 85.2 %copy-start.9 = (bf16[512,16]{0,1:T(8,128)(2,1)S(1)}, bf16[512,16]{0,1:T(8,128)(2,1)}, u32[]{:S(2)}) copy-start(bf16[512,16]{0,1:T(8,128)(2,1)} %copy-done.8) | copy-start | bytes 49156
  336.6 86.7 %copy-start.1 = (bf16[16,16,4608]{2,1,0:T(8,128)(2,1)S(1)}, bf16[16,16,4608]{2,1,0:T(8,128)(2,1)}, u32[]{:S(2)}) copy-start(bf16[16,16,4608]{2,1,0:T(8,128)(2,1)} %param.18) | copy-start | bytes 7077892
Sparse Core Ops, SparseCore 0:
  9.7 52.7 all-gather.8
  65.2 123.6 all-gather.4
  252.3 78.6 all-gather.6
  333.2 86.3 reduce-scatter.1

commit v2 on v0

v2 whole, which is shorter than its diff:
```python
import math

import jax
import jax.numpy as jnp
from jax import lax
from jax.experimental import pallas as pl
from jax.experimental.pallas import tpu as pltpu
from jax.sharding import PartitionSpec as P

D = 4608
HD = 128
TOKENS = 512
RANK = 16
ADAPTERS = 16
SIDE = 4
ROWS = 288
GROUP = 512
COLS = 1152
TERM = 3840
BLOCK = TERM + 128

soft_cap = 50.0
adapter_scale = 2.0
score_scale = 1.0 / 12.0

MESH = pl.DeviceIdType.MESH
F32 = jnp.float32
BF16 = jnp.bfloat16
VMEM_BYTES = 60 * 1024 * 1024


def dot(a, b, dims):
    return lax.dot_general(a, b, (dims, ((), ())), preferred_element_type=F32)


class Place:
    def __init__(self):
        self.dp = lax.axis_index("dp")
        self.f = lax.axis_index("fsdp")
        self.t = lax.axis_index("tensor")
        self.y, self.z = self.f // SIDE, self.f % SIDE
        self.core = self.t % 2
        self.x = self.dp * 2 + self.t // 2

    def at_x(self, x, core):
        return (x // 2, self.f, (x % 2) * 2 + core)

    def step_x(self, n):
        return (self.x + n) % SIDE

    def ring_x(self, n):
        return self.at_x(self.step_x(n), self.core)

    def sibling(self):
        return self.at_x(self.x, 1 - self.core)

    def ring_y(self, n):
        return (self.dp, ((self.y + n) % SIDE) * SIDE + self.z, self.t)

    def ring_z(self, n):
        return (self.dp, self.y * SIDE + (self.z + n) % SIDE, self.t)


class Net:
    def __init__(self, send_sems, recv_sems):
        self.send_sems, self.recv_sems = send_sems, recv_sems
        self.started = []

    def send(self, index, src, dst, device):
        copy = pltpu.make_async_remote_copy(
            src_ref=src,
            dst_ref=dst,
            send_sem=self.send_sems.at[index],
            recv_sem=self.recv_sems.at[index],
            device_id=device,
            device_id_type=MESH,
        )
        copy.start()
        self.started.append(copy)

    def arrived(self, index, region, device):
        pltpu.make_async_remote_copy(
            src_ref=region,
            dst_ref=region,
            send_sem=self.send_sems.at[index],
            recv_sem=self.recv_sems.at[index],
            device_id=device,
            device_id_type=MESH,
        ).wait_recv()

    def finish(self):
        for copy in self.started:
            copy.wait_send()


def enter(peers):
    barrier = pltpu.get_barrier_semaphore()
    for peer in peers:
        pl.semaphore_signal(barrier, inc=1, device_id=peer, device_id_type=MESH)
    pl.semaphore_wait(barrier, len(peers))


class TorusGather:
    def __init__(self, net, base, place, y_first, view, whole, low, high):
        self.net, self.base = net, base
        self.whole, self.low, self.high = whole, low, high
        p = place
        if y_first:
            self.one, self.two = p.ring_y, p.ring_z
            self.block = lambda n, w: view((p.y + n) % SIDE, p.z, w)
            self.line = lambda n, w: view(None, (p.z + n) % SIDE, w)
        else:
            self.one, self.two = p.ring_z, p.ring_y
            self.block = lambda n, w: view(p.y, (p.z + n) % SIDE, w)
            self.line = lambda n, w: view((p.y + n) % SIDE, None, w)

    def fan(self, base, region, ring):
        own = region(0, self.whole)
        self.net.send(base, own, own, ring(1))
        self.net.send(base + 1, own, own, ring(-1))

    def forward(self, base, region, ring):
        self.net.arrived(base, region(-1, self.whole), ring(-1))
        part = region(-1, self.low)
        self.net.send(base + 2, part, part, ring(1))
        self.net.arrived(base + 1, region(1, self.whole), ring(1))
        part = region(1, self.high)
        self.net.send(base + 3, part, part, ring(-1))

    def close(self, base, region, ring):
        self.net.arrived(base + 2, region(2, self.low), ring(-1))
        self.net.arrived(base + 3, region(2, self.high), ring(1))

    def stage(self, n):
        if n == 1:
            self.fan(self.base, self.block, self.one)
        elif n == 2:
            self.forward(self.base, self.block, self.one)
        elif n == 3:
            self.close(self.base, self.block, self.one)
            self.fan(self.base + 4, self.line, self.two)
        elif n == 4:
            self.forward(self.base + 4, self.line, self.two)
        else:
            self.close(self.base + 4, self.line, self.two)


def gather_kernel(
    x_ref, g_ref, wq_ref, wk_ref, wv_ref, meta_ref, qd_ref, vd_ref, qu_ref, vu_ref,
    w_out, qkv_out, low_out, up_out, down_out, g_out, meta_out,
    xs, ws, qds, vds, down, send_sems, recv_sems, local_sems, first_sems,
):
    p = Place()
    net = Net(send_sems, recv_sems)
    my_cols = pl.ds(pl.multiple_of(p.t * COLS, COLS), COLS)
    half = lambda ref, dp, width: ref.at[:, pl.ds(pl.multiple_of(dp * width, width), width)]

    first = [pltpu.make_async_copy(x_ref, xs.at[p.dp, :, my_cols], first_sems.at[0])]
    for g in range(2):
        c0 = g * GROUP
        for n, (ref, at, width) in enumerate(
            ((wq_ref, c0, 256), (wk_ref, c0 + 256, 128), (wv_ref, c0 + 384, 128))
        ):
            source = ref.at[:, pl.ds(pl.multiple_of(p.dp * 2 * width + g * width, width), width)]
            first.append(
                pltpu.make_async_copy(
                    source,
                    ws.at[p.y, pl.ds(pl.multiple_of(p.z * ROWS, 32), ROWS), at : at + width],
                    first_sems.at[1 + 3 * g + n],
                )
            )
    for copy in first:
        copy.start()
    later = [
        pltpu.make_async_copy(qd_ref, qds, local_sems.at[0]),
        pltpu.make_async_copy(vd_ref, vds, local_sems.at[1]),
        pltpu.make_async_copy(half(g_ref, p.dp, 512), g_out.at[p.dp], local_sems.at[2]),
    ]
    for copy in later:
        copy.start()
    meta_out[p.dp] = meta_ref[...]

    partner = p.ring_x(2)
    enter([
        p.ring_x(1), p.ring_x(-1), partner, p.sibling(),
        p.ring_y(1), p.ring_y(-1), p.ring_z(1), p.ring_z(-1),
    ])

    def x_block(n, core, rows=slice(None)):
        chip = p.step_x(n)
        column = pl.multiple_of(((chip % 2) * 2 + core) * COLS, COLS)
        return xs.at[chip // 2, rows, pl.ds(column, COLS)]

    upper, lower = slice(0, 256), slice(256, 512)
    net.send(0, meta_out.at[p.dp], meta_out.at[p.dp], partner)
    for copy in first:
        copy.wait()

    def view(y, z, window):
        rows = slice(None) if z is None else pl.ds(pl.multiple_of(z * ROWS, 32), ROWS)
        return ws.at[slice(None) if y is None else y, rows, window]

    gathers = []
    for g in range(2):
        for h in range(2):
            c = g * GROUP + h * 256
            gathers.append(
                TorusGather(
                    net, 16 + 8 * (2 * g + h), p, h == 0, view,
                    slice(c, c + 256), slice(c, c + 128), slice(c + 128, c + 256),
                )
            )

    def weights(g, stage):
        for one in gathers[2 * g : 2 * g + 2]:
            one.stage(stage)

    own = x_block(0, p.core)
    weights(0, 1)
    net.send(1, own, own, p.ring_x(1))
    net.send(2, own, own, p.ring_x(-1))
    net.send(3, own, own, p.sibling())
    net.send(4, half(g_ref, 1 - p.dp, 512), g_out.at[p.dp], partner)
    weights(0, 2)
    weights(1, 1)
    weights(0, 3)
    weights(1, 2)

    for copy in later:
        copy.wait()
    net.arrived(0, meta_out.at[1 - p.dp], partner)
    up_out[...] = jnp.zeros_like(up_out)
    for s in range(2):
        chosen = meta_out[s, 0:1, 0:1]

        def add(a, sums):
            weight = (chosen == a).astype(F32)
            return (
                sums[0] + qds[a].astype(F32) * weight,
                sums[1] + vds[a].astype(F32) * weight,
                sums[2] + qu_ref[a].astype(F32) * weight,
                sums[3] + vu_ref[a].astype(F32) * weight,
            )

        zero = lambda width: jnp.zeros((RANK, width), F32)
        q_rows, v_rows, q_up, v_up = lax.fori_loop(
            0, ADAPTERS, add, (zero(D), zero(D), zero(512), zero(256))
        )
        down[s, :RANK, :] = q_rows.astype(BF16)
        down[s, RANK:, :] = v_rows.astype(BF16)
        for g in range(2):
            c0 = g * GROUP
            up_out[s, :RANK, c0 : c0 + 256] = q_up[:, g * 256 : g * 256 + 256].astype(BF16)
            up_out[s, RANK:, c0 + 384 : c0 + 512] = v_up[:, g * 128 : g * 128 + 128].astype(BF16)
    down_out[...] = down[p.dp, :, my_cols]

    net.arrived(1, x_block(-1, p.core), p.ring_x(-1))
    part = x_block(-1, p.core, upper)
    net.send(5, part, part, p.ring_x(1))
    part = x_block(-1, p.core)
    net.send(6, part, part, p.sibling())
    net.arrived(2, x_block(1, p.core), p.ring_x(1))
    part = x_block(1, p.core, lower)
    net.send(7, part, part, p.ring_x(-1))
    part = x_block(1, p.core)
    net.send(8, part, part, p.sibling())
    weights(0, 4)
    weights(1, 3)
    net.arrived(5, x_block(2, p.core, upper), p.ring_x(-1))
    part = x_block(2, p.core, upper)
    net.send(9, part, part, p.sibling())
    net.arrived(7, x_block(2, p.core, lower), p.ring_x(1))
    part = x_block(2, p.core, lower)
    net.send(10, part, part, p.sibling())
    other = 1 - p.core
    net.arrived(3, x_block(0, other), p.sibling())
    net.arrived(6, x_block(-1, other), p.sibling())
    net.arrived(8, x_block(1, other), p.sibling())
    net.arrived(9, x_block(2, other, upper), p.sibling())
    net.arrived(10, x_block(2, other, lower), p.sibling())
    weights(0, 5)
    weights(1, 4)

    @pl.loop(0, 2)
    def _(s):
        low_out[s] = dot(xs[s], down[s], ((1,), (1,))).astype(BF16)

    def project(g):
        @pl.loop(0, 4)
        def _(n):
            s = n // 2
            window = pl.ds(pl.multiple_of(g * GROUP + (n % 2) * 256, 256), 256)
            base = dot(xs[s], ws[:, :, window].reshape(D, 256), ((1,), (0,)))
            extra = dot(low_out[s], up_out[s, :, window], ((1,), (0,)))
            qkv_out[s, :, window] = (base + adapter_scale * extra).astype(BF16)

    project(0)
    weights(1, 5)
    save = pltpu.make_async_copy(ws, w_out, local_sems.at[3])
    save.start()
    project(1)
    net.arrived(4, g_out.at[1 - p.dp], partner)
    net.finish()
    save.wait()


def gather_call(x, g, wq, wk, wv, meta, qd, vd, qu, vu):
    hbm = pl.BlockSpec(memory_space=pl.ANY)
    vmem = pl.BlockSpec(memory_space=pltpu.VMEM)
    return pl.pallas_call(
        gather_kernel,
        name="gather_project",
        out_shape=(
            jax.ShapeDtypeStruct((SIDE, COLS, 2 * GROUP), BF16),
            jax.ShapeDtypeStruct((2, TOKENS, 2 * GROUP), BF16),
            jax.ShapeDtypeStruct((2, TOKENS, 2 * RANK), BF16),
            jax.ShapeDtypeStruct((2, 2 * RANK, 2 * GROUP), BF16),
            jax.ShapeDtypeStruct((2 * RANK, COLS), BF16),
            jax.ShapeDtypeStruct((2, TOKENS, 512), BF16),
            jax.ShapeDtypeStruct((2, 8, 128), jnp.int32),
        ),
        in_specs=[hbm] * 5 + [vmem, hbm, hbm, vmem, vmem],
        out_specs=(hbm, vmem, vmem, vmem, vmem, hbm, vmem),
        scratch_shapes=[
            pltpu.VMEM((2, TOKENS, D), BF16),
            pltpu.VMEM((SIDE, COLS, 2 * GROUP), BF16),
            pltpu.VMEM((ADAPTERS, RANK, D), BF16),
            pltpu.VMEM((ADAPTERS, RANK, D), BF16),
            pltpu.VMEM((2, 2 * RANK, D), BF16),
            pltpu.SemaphoreType.DMA((48,)),
            pltpu.SemaphoreType.DMA((48,)),
            pltpu.SemaphoreType.DMA((4,)),
            pltpu.SemaphoreType.DMA((7,)),
        ],
        compiler_params=pltpu.CompilerParams(
            collective_id=0, has_side_effects=True, vmem_limit_bytes=VMEM_BYTES
        ),
    )(x, g, wq, wk, wv, meta, qd, vd, qu, vu)


def attention_kernel(
    qkv_ref, cot_ref, low_ref, up_ref, meta_ref, d_ref, dlow_ref, term_ref, dk_acc, dv_acc
):
    s, g = pl.program_id(0), pl.program_id(1)
    length = meta_ref[0, 1:2, 0:1]
    k = qkv_ref[0, :, 256:384]
    v = qkv_ref[0, :, 384:512]
    dk_acc[...] = jnp.zeros_like(dk_acc)
    dv_acc[...] = jnp.zeros_like(dv_acc)
    step = 256
    for ib in range(TOKENS // step):
        rows = slice(ib * step, (ib + 1) * step)
        span = (ib + 1) * step
        key_at = lax.broadcasted_iota(jnp.int32, (span, step), 0)
        row_at = lax.broadcasted_iota(jnp.int32, (span, step), 1) + ib * step
        allowed = (key_at <= row_at) & (key_at < length)
        used = lax.broadcasted_iota(jnp.int32, (step, HD), 0) + ib * step < length
        for h in range(2):
            head = slice(h * HD, (h + 1) * HD)
            q = qkv_ref[0, rows, head]
            cot = cot_ref[0, rows, head]
            cot = jnp.where(used, cot, jnp.zeros_like(cot))
            raw = dot(k[:span], q, ((1,), (1,)))
            turned = jnp.tanh(raw * (score_scale / soft_cap))
            weights = jnp.where(allowed, jnp.exp(soft_cap * turned), 0.0)
            probs = weights * (1.0 / jnp.sum(weights, axis=0, keepdims=True))
            probs_b = probs.astype(BF16)
            dprob = dot(v[:span], cot, ((1,), (1,)))
            row_total = jnp.sum(probs * dprob, axis=0, keepdims=True)
            dscore = (
                probs * (dprob - row_total) * ((1.0 - turned * turned) * score_scale)
            ).astype(BF16)
            dq = dot(k[:span], dscore, ((0,), (0,)))
            d_ref[0, rows, head] = dq.T.astype(BF16)
            dk_acc[:span] += dot(dscore, q, ((1,), (0,)))
            dv_acc[:span] += dot(probs_b, cot, ((1,), (0,)))
    d_ref[0, :, 256:384] = dk_acc[...].astype(BF16)
    d_ref[0, :, 384:512] = dv_acc[...].astype(BF16)
    grads = d_ref[0]
    dlow = adapter_scale * dot(up_ref[0], grads, ((1,), (1,)))

    @pl.when(g == 0)
    def _():
        dlow_ref[0] = dlow

    @pl.when(g == 1)
    def _():
        dlow_ref[0] += dlow

    terms = (adapter_scale * dot(low_ref[0], grads, ((0,), (0,)))).astype(BF16)
    q_at = pl.multiple_of(s * 512 + g * 256, 256)
    v_at = pl.multiple_of(1024 + s * 256 + g * 128, 128)
    term_ref[:, pl.ds(q_at, 256)] = terms[:RANK, 0:256]
    term_ref[:, pl.ds(v_at, 128)] = terms[RANK:, 384:512]


def attention_call(qkv, cot, low, up, meta):
    return pl.pallas_call(
        attention_kernel,
        name="attention",
        grid=(2, 2),
        out_shape=(
            jax.ShapeDtypeStruct((2, TOKENS, 2 * GROUP), BF16),
            jax.ShapeDtypeStruct((2, 2 * RANK, TOKENS), F32),
            jax.ShapeDtypeStruct((RANK, 1536), BF16),
        ),
        in_specs=[
            pl.BlockSpec((1, TOKENS, GROUP), lambda s, g: (s, 0, g)),
            pl.BlockSpec((1, TOKENS, 256), lambda s, g: (s, 0, g)),
            pl.BlockSpec((1, TOKENS, 2 * RANK), lambda s, g: (s, 0, 0)),
            pl.BlockSpec((1, 2 * RANK, GROUP), lambda s, g: (s, 0, g)),
            pl.BlockSpec((1, 8, 128), lambda s, g: (s, 0, 0)),
        ],
        out_specs=(
            pl.BlockSpec((1, TOKENS, GROUP), lambda s, g: (s, 0, g)),
            pl.BlockSpec((1, 2 * RANK, TOKENS), lambda s, g: (s, 0, 0)),
            pl.BlockSpec((RANK, 1536), lambda s, g: (0, 0)),
        ),
        scratch_shapes=[pltpu.VMEM((TOKENS, HD), F32), pltpu.VMEM((TOKENS, HD), F32)],
        compiler_params=pltpu.CompilerParams(
            dimension_semantics=("arbitrary", "arbitrary"), vmem_limit_bytes=VMEM_BYTES
        ),
    )(qkv, cot, low, up, meta)


def scatter_kernel(
    d_ref, w_ref, x_ref, dlow_ref, up_term_ref, down_ref, tag_ref,
    grad_out, table_out,
    ws, sib_out, sib_in, ring_out, relay_in, ring_in, chip_low, sib_low, low_in, tables,
    send_sems, recv_sems, local_sems,
):
    p = Place()
    net = Net(send_sems, recv_sems)
    load = pltpu.make_async_copy(w_ref, ws, local_sems.at[0])
    load.start()
    partner = p.ring_x(2)
    sib = p.sibling()
    enter([
        p.ring_x(1), p.ring_x(-1), partner, sib,
        p.ring_y(1), p.ring_y(-1), p.ring_z(1), p.ring_z(-1),
    ])
    net.send(0, dlow_ref, sib_low, sib)

    chunk = 384

    def for_sibling(slot, n):
        chip = p.step_x(n)
        part = (chip % 2) * 2 + 1 - p.core
        for c in range(0, COLS, chunk):
            value = dot(d_ref[chip // 2], ws[part, c : c + chunk], ((1,), (1,)))
            sib_out[slot, :, c : c + chunk] = value.astype(BF16)
        net.send(1 + slot, sib_out.at[slot], sib_in.at[slot], sib)

    def own_core(slot, n):
        chip = p.step_x(n)
        part = (chip % 2) * 2 + p.core
        net.arrived(1 + slot, sib_in.at[slot], sib)
        for c in range(0, COLS, chunk):
            cols = slice(c, c + chunk)
            value = dot(d_ref[chip // 2], ws[part, cols], ((1,), (1,)))
            yield cols, value + sib_in[slot, :, cols].astype(F32)

    upper, lower = slice(0, 256), slice(256, 512)
    load.wait()
    for_sibling(0, 2)
    for_sibling(1, 1)
    net.arrived(0, sib_low, sib)
    chip_low[...] = dlow_ref[...] + sib_low[...]
    for n in (1, 2, 3):
        net.send(4 + n, chip_low.at[p.step_x(n) // 2], low_in.at[n - 1], p.ring_x(n))
    for cols, value in own_core(0, 2):
        ring_out[0, :, cols] = value.astype(BF16)
    net.send(8, ring_out.at[0, upper], relay_in.at[0], p.ring_x(1))
    net.send(9, ring_out.at[0, lower], relay_in.at[1], p.ring_x(-1))
    for_sibling(2, -1)
    for cols, value in own_core(1, 1):
        ring_out[1, :, cols] = value.astype(BF16)
    net.send(10, ring_out.at[1, lower], ring_in.at[0, lower], p.ring_x(1))
    for cols, value in own_core(2, -1):
        ring_out[2, :, cols] = value.astype(BF16)
    net.send(11, ring_out.at[2, upper], ring_in.at[1, upper], p.ring_x(-1))
    for_sibling(3, 0)

    total = chip_low[p.dp]
    for n in (1, 2, 3):
        net.arrived(4 + n, low_in.at[n - 1], p.ring_x(-n))
        total = total + low_in[n - 1]
    low_grad = total.astype(BF16)
    down_terms = dot(low_grad, x_ref[...], ((1,), (0,))).astype(BF16)
    mine = tables.at[p.dp, p.y, p.z]
    mine[:, 0:COLS] = down_terms[:RANK]
    mine[:, COLS : 2 * COLS] = down_terms[RANK:]
    mine[:, 2 * COLS : TERM] = up_term_ref[...]
    mine[:, TERM:] = tag_ref[...]
    net.send(14, mine, mine, partner)

    net.arrived(8, relay_in.at[0], p.ring_x(-1))
    ring_out[1, upper] = (ring_out[1, upper].astype(F32) + relay_in[0].astype(F32)).astype(BF16)
    net.send(12, ring_out.at[1, upper], ring_in.at[0, upper], p.ring_x(1))
    net.arrived(9, relay_in.at[1], p.ring_x(1))
    ring_out[2, lower] = (ring_out[2, lower].astype(F32) + relay_in[1].astype(F32)).astype(BF16)
    net.send(13, ring_out.at[2, lower], ring_in.at[1, lower], p.ring_x(-1))

    def view(y, z, window):
        everything = slice(None)
        return tables.at[
            :, everything if y is None else y, everything if z is None else z, :, window
        ]

    gathers = [
        TorusGather(net, 16, p, True, view, slice(0, 2048), slice(0, 1024), slice(1024, 2048)),
        TorusGather(
            net, 24, p, False, view, slice(2048, BLOCK), slice(2048, 3072), slice(3072, BLOCK)
        ),
    ]
    net.arrived(14, tables.at[1 - p.dp, p.y, p.z], partner)
    for one in gathers:
        one.stage(1)
    low_part = dot(low_grad, down_ref[...], ((0,), (0,)))
    kept = []
    for cols, value in own_core(3, 0):
        kept.append((cols, value + low_part[:, cols]))
    for stage in (2, 3, 4):
        for one in gathers:
            one.stage(stage)
    net.arrived(10, ring_in.at[0, lower], p.ring_x(-1))
    net.arrived(11, ring_in.at[1, upper], p.ring_x(1))
    net.arrived(12, ring_in.at[0, upper], p.ring_x(-1))
    net.arrived(13, ring_in.at[1, lower], p.ring_x(1))
    for cols, value in kept:
        value = value + ring_in[0, :, cols].astype(F32) + ring_in[1, :, cols].astype(F32)
        grad_out[:, cols] = value.astype(BF16)
    for one in gathers:
        one.stage(5)
    save = pltpu.make_async_copy(tables, table_out, local_sems.at[1])
    save.start()
    net.finish()
    save.wait()


def scatter_call(d, w, x, dlow, up_terms, down, tag):
    hbm = pl.BlockSpec(memory_space=pl.ANY)
    vmem = pl.BlockSpec(memory_space=pltpu.VMEM)
    return pl.pallas_call(
        scatter_kernel,
        name="scatter_sum",
        out_shape=(
            jax.ShapeDtypeStruct((TOKENS, COLS), BF16),
            jax.ShapeDtypeStruct((2, SIDE, SIDE, RANK, BLOCK), BF16),
        ),
        in_specs=[vmem, hbm, vmem, vmem, vmem, vmem, vmem],
        out_specs=(vmem, hbm),
        scratch_shapes=[
            pltpu.VMEM((SIDE, COLS, 2 * GROUP), BF16),
            pltpu.VMEM((4, TOKENS, COLS), BF16),
            pltpu.VMEM((4, TOKENS, COLS), BF16),
            pltpu.VMEM((3, TOKENS, COLS), BF16),
            pltpu.VMEM((2, 256, COLS), BF16),
            pltpu.VMEM((2, TOKENS, COLS), BF16),
            pltpu.VMEM((2, 2 * RANK, TOKENS), F32),
            pltpu.VMEM((2, 2 * RANK, TOKENS), F32),
            pltpu.VMEM((3, 2 * RANK, TOKENS), F32),
            pltpu.VMEM((2, SIDE, SIDE, RANK, BLOCK), BF16),
            pltpu.SemaphoreType.DMA((32,)),
            pltpu.SemaphoreType.DMA((32,)),
            pltpu.SemaphoreType.DMA((2,)),
        ],
        compiler_params=pltpu.CompilerParams(
            collective_id=1, has_side_effects=True, vmem_limit_bytes=VMEM_BYTES
        ),
    )(d, w, x, dlow, up_terms, down, tag)


def shards(
    x_in, lengths, adapter_ids, attn_grad, w_query, w_key, w_value,
    query_down, query_up, value_down, value_up,
):
    dp = lax.axis_index("dp")
    meta = jnp.zeros((8, 128), jnp.int32).at[0].set(adapter_ids[0]).at[1].set(lengths[0])
    tag = jnp.full((RANK, 128), adapter_ids[0], jnp.int32).astype(BF16)
    q_up = lax.dynamic_slice_in_dim(query_up, dp * 512, 512, 2)
    v_up = lax.dynamic_slice_in_dim(value_up, dp * 256, 256, 2)
    w_all, qkv, low, up, down, cot, meta_both = gather_call(
        x_in[0], attn_grad[0], w_query, w_key, w_value, meta,
        query_down, value_down, q_up, v_up,
    )
    grads, dlow, up_terms = attention_call(qkv, cot, low, up, meta_both)
    grad_input, blocks = scatter_call(grads, w_all, x_in[0], dlow, up_terms, down, tag)

    ids = blocks[:, :, :, 0, TERM].reshape(2, 16)
    owners = (ids[:, :, None] == lax.iota(jnp.int32, ADAPTERS).astype(BF16)).astype(BF16)
    blocks = blocks.reshape(2, 16, RANK, BLOCK)
    down_terms = blocks[..., : 2 * COLS]
    down_tables = jnp.einsum("dfa,dfrc->arc", owners, down_terms, preferred_element_type=F32)
    q_terms = blocks[..., 2 * COLS : 2 * COLS + 1024].reshape(2, 16, RANK, 2, 512)
    q_tables = jnp.einsum("sfa,dfrsc->ardc", owners, q_terms, preferred_element_type=F32)
    v_terms = blocks[..., 2 * COLS + 1024 : TERM].reshape(2, 16, RANK, 2, 256)
    v_tables = jnp.einsum("sfa,dfrsc->ardc", owners, v_terms, preferred_element_type=F32)
    return (
        grad_input[None],
        down_tables[..., :COLS],
        q_tables.reshape(ADAPTERS, RANK, 1024),
        down_tables[..., COLS:],
        v_tables.reshape(ADAPTERS, RANK, 512),
    )


def solution(mesh):
    placed = (
        P(("dp", "fsdp"), None, "tensor"),
        P(("dp", "fsdp")),
        P(("dp", "fsdp")),
        P(("dp", "fsdp"), None, "tensor"),
        P("fsdp", "tensor"),
        P("fsdp", "tensor"),
        P("fsdp", "tensor"),
        P(),
        P(None, None, "tensor"),
        P(),
        P(None, None, "tensor"),
    )
    return jax.shard_map(
        shards,
        mesh=mesh,
        in_specs=placed,
        out_specs=(
            P(("dp", "fsdp"), None, "tensor"),
            P(None, None, "tensor"),
            P(None, None, "tensor"),
            P(None, None, "tensor"),
            P(None, None, "tensor"),
        ),
        check_vma=False,
    )
```

time: 805 us -> 189 us (0.23)
  waiting for transfers between devices: 644 us -> 0 us
  Pallas kernels: 0 us -> 165 us
  matrix products: 114 us -> 2.67 us
  between operations: 15.6 us -> 2.07 us
  blocking collectives: 12.5 us -> 0 us
    psum x1 -> x0, waiting for transfers between devices: 365 us -> none  [shards(): lax.psum((owner_row[:, None, None] * term_qa[None], owner_row[:, None, No...]
    all_gather x4 -> x0, waiting for transfers between devices: 207 us -> none  [the longest x1 70.9 us: shards(): lax.all_gather(w_query, 'fsdp', axis=0, tiled=True)]
    pallas_call x0 -> x3, Pallas kernels: none -> 165 us  [the longest x1 78.6 us: gather_call(): pl.pallas_call(gather_kernel, name='gather_project', out_shape=(jax.Shape...]
    dot_general x27 -> x3, matrix products: 114 us -> 2.67 us  [the longest x1 1.46 us: shards(): jnp.einsum('dfa,dfrc->arc', owners, down_terms, preferred_element_type=F32)]
    reduce_scatter x1 -> x0, waiting for transfers between devices: 69.5 us -> none  [shards(): lax.psum_scatter(partial_value, 'tensor', scatter_dimension=1, tiled=True)]
    psum x1 -> x0, blocking collectives: 12.5 us -> none  [shards(): sum_q, sum_v = lax.psum((query_portion, value_portion), 'tensor')]
  transfers between devices with their start and end apart: 6 -> 0, of which waited for: 6 -> 0; matrix products, arithmetic and copies ran while one was open for 6% -> 0% of each run, Pallas kernels for 0% -> 0%
where the time goes in v2:
time: 189 us
  Pallas kernels  165 us (87%)
  local copies, waits for them, and re-layouts  19 us (10%)
  matrix products  2.67 us (1%)
  between operations  2.07 us (1%)
    pallas_call x1, Pallas kernels, gather_call(): pl.pallas_call(gather_kernel, name='gather_project', out_shape=(jax.Shape...  78.6 us
    pallas_call x1, Pallas kernels, scatter_call(): pl.pallas_call(scatter_kernel, name='scatter_sum', out_shape=(jax.ShapeDt...  73.5 us
    pallas_call x1, Pallas kernels, attention_call(): pl.pallas_call(attention_kernel, name='attention', grid=(2, 2), out_shape...  12.7 us
    unnamed x9, local copies, waits for them, and re-layouts  5.39 us

profile of v2, /device:TPU:0, one launch (start us, length us, event | category | flops | bytes accessed | tf_op | source)
XLA Modules:
  0.0 188.5 jit_solution(11381149339475934982)
XLA Ops:
  0.6 0.0 copy-start
  0.7 1.0 copy-done
  1.7 0.7 constant_dynamic-slice_fusion.1.qu_ref
  2.4 1.6 constant_dynamic-slice_fusion.vu_ref
  4.6 0.1 scatter.13
  5.4 0.0 copy-start.2
  5.4 0.6 copy-done.2
  6.0 78.6 %gather_project.1 = (bf16[4,1152,1024]{2,1,0:T(8,128)(2,1)}, bf16[2,512,1024]{2,1,0:T(8,128)(2,1)}, bf16[2,512,32]{2,1,0:T(8,128)(2,1)}, bf16[2,32,1024]{2,1,0:T...) custom-call(bf16[512,1152]{1,0:T(8,128)(2,1)} %bitcast.33, ...), custom_call_target="tpu_custom_call" | custom-call | tf_op jit(solution)/shard_map/gather_project/pallas_call | solution.py:310
  84.6 12.7 %attention.1 = (bf16[2,512,1024]{2,1,0:T(8,128)(2,1)}, f32[2,32,512]{2,1,0:T(8,128)}, bf16[16,1536]{1,0:T(8,128)(2,1)}) custom-call(bf16[2,512,1024]{2,1,0:T(8,128)(2,1)} %get-tuple-element.41.qkv_ref, bf16[2,512,512]{2,1,0:T(8,128)(2,1)} %get-tuple-element.42.cot_ref, bf16[2,512,32]{2,1,0:T(8,128)(2,1)} %get-tuple-element.43.low_ref, ...), custom_call_target="tpu_custom_call" | custom-call | tf_op jit(solution)/shard_map/attention/pallas_call | solution.py:398
  97.3 0.6 broadcast_in_dim.4.tag_ref
  97.9 73.5 %scatter_sum.1 = (bf16[512,1152]{1,0:T(8,128)(2,1)}, bf16[2,4,4,16,3968]{4,3,2,1,0:T(8,128)(2,1)}) custom-call(bf16[2,512,1024]{2,1,0:T(8,128)(2,1)} %get-tuple-element.46.d_ref, bf16[4,1152,1024]{2,1,0:T(8,128)(2,1)} %get-tuple-element.47.w_ref, bf16[512,1152]{1,0:T(8,128)(2,1)} %bitcast.34, f32[2,32,512]{2,1,0:T(8,128)} %get-tuple-element.48.dlow_ref, ...), custom_call_target="tpu_custom_call" | custom-call | tf_op jit(solution)/shard_map/scatter_sum/pallas_call | solution.py:544
  171.4 1.1 slice.56
  172.4 0.1 reshape.77
  172.6 1.0 slice_reduce_fusion
  173.6 0.1 eq.15
  173.7 0.5 convolution_bitcast_fusion.2
  174.1 0.4 copy.23
  174.5 1.2 reshape.78
  175.7 1.3 slice.54
  177.1 0.8 reshape.75
  177.9 0.7 convolution_bitcast_fusion.1
  178.6 0.8 copy.21
  179.4 1.9 reshape.76
  181.3 1.8 slice.52
  183.1 1.5 convolution_bitcast_fusion
  184.6 0.2 fusion.9
  184.7 0.0 copy-start.1
  184.7 1.4 copy.24
  186.1 1.4 copy.25
  187.5 0.0 copy-done.1
  187.5 1.0 copy.41
  (4 shorter events, 0.0 us)
Async XLA Ops:
  0.6 1.0 copy-start
  5.4 0.6 copy-start.2
  184.7 2.8 %copy-start.1 = (bf16[512,1152]{1,0:T(8,128)(2,1)S(1)}, bf16[512,1152]{1,0:T(8,128)(2,1)}, u32[]{:S(2)}) copy-start(bf16[512,1152]{1,0:T(8,128)(2,1)} %get-tuple-element.51) | copy-start | bytes 3538948

commit v3 on v0

v3 whole, which is shorter than its diff:
```python
import math

import jax
import jax.numpy as jnp
from jax import lax
from jax.experimental import pallas as pl
from jax.experimental.pallas import tpu as pltpu
from jax.sharding import PartitionSpec as P

D = 4608
HD = 128
TOKENS = 512
RANK = 16
ADAPTERS = 16
SIDE = 4
ROWS = 288
GROUP = 512
COLS = 1152
HALF = 256
UP = 1536 + 128
DOWN = 2 * COLS

soft_cap = 50.0
adapter_scale = 2.0
score_scale = 1.0 / 12.0

MESH = pl.DeviceIdType.MESH
F32 = jnp.float32
BF16 = jnp.bfloat16
VMEM_BYTES = 60 * 1024 * 1024


def dot(a, b, dims):
    return lax.dot_general(a, b, (dims, ((), ())), preferred_element_type=F32)


class Place:
    def __init__(self):
        self.dp = lax.axis_index("dp")
        self.f = lax.axis_index("fsdp")
        self.t = lax.axis_index("tensor")
        self.y, self.z = self.f // SIDE, self.f % SIDE
        self.core = self.t % 2
        self.x_lo = self.t // 2
        x = self.dp * 2 + self.x_lo
        to_mate = 1 - 2 * self.x_lo
        at = lambda n, core: ((n % SIDE) // 2, self.f, (n % 2) * 2 + core)
        self.mate = at(x + to_mate + SIDE, self.core)
        self.cross = at(x - to_mate + SIDE, self.core)
        self.opposite = at(x + 2, self.core)
        self.sibling = at(x, 1 - self.core)

    def part(self, flip, core):
        return ((self.x_lo + flip) % 2) * 2 + core

    def ring_y(self, n):
        return (self.dp, ((self.y + n) % SIDE) * SIDE + self.z, self.t)

    def ring_z(self, n):
        return (self.dp, self.y * SIDE + (self.z + n) % SIDE, self.t)


class Net:
    def __init__(self, send_sems, recv_sems):
        self.send_sems, self.recv_sems = send_sems, recv_sems
        self.started = []

    def send(self, index, src, dst, device):
        copy = pltpu.make_async_remote_copy(
            src_ref=src,
            dst_ref=dst,
            send_sem=self.send_sems.at[index],
            recv_sem=self.recv_sems.at[index],
            device_id=device,
            device_id_type=MESH,
        )
        copy.start()
        self.started.append(copy)

    def arrived(self, index, region, device):
        pltpu.make_async_remote_copy(
            src_ref=region,
            dst_ref=region,
            send_sem=self.send_sems.at[index],
            recv_sem=self.recv_sems.at[index],
            device_id=device,
            device_id_type=MESH,
        ).wait_recv()

    def finish(self):
        for copy in self.started:
            copy.wait_send()


def enter(peers):
    barrier = pltpu.get_barrier_semaphore()
    for peer in peers:
        pl.semaphore_signal(barrier, inc=1, device_id=peer, device_id_type=MESH)
    pl.semaphore_wait(barrier, len(peers))


class TorusGather:
    def __init__(self, net, base, place, y_first, view, whole, low, high):
        self.net, self.base = net, base
        self.whole, self.low, self.high = whole, low, high
        p = place
        if y_first:
            self.one, self.two = p.ring_y, p.ring_z
            self.block = lambda n, w: view((p.y + n) % SIDE, p.z, w)
            self.line = lambda n, w: view(None, (p.z + n) % SIDE, w)
        else:
            self.one, self.two = p.ring_z, p.ring_y
            self.block = lambda n, w: view(p.y, (p.z + n) % SIDE, w)
            self.line = lambda n, w: view((p.y + n) % SIDE, None, w)

    def fan(self, base, region, ring):
        own = region(0, self.whole)
        self.net.send(base, own, own, ring(1))
        self.net.send(base + 1, own, own, ring(-1))

    def forward(self, base, region, ring):
        self.net.arrived(base, region(-1, self.whole), ring(-1))
        part = region(-1, self.low)
        self.net.send(base + 2, part, part, ring(1))
        self.net.arrived(base + 1, region(1, self.whole), ring(1))
        part = region(1, self.high)
        self.net.send(base + 3, part, part, ring(-1))

    def close(self, base, region, ring):
        self.net.arrived(base + 2, region(2, self.low), ring(-1))
        self.net.arrived(base + 3, region(2, self.high), ring(1))

    def stage(self, n):
        if n == 1:
            self.fan(self.base, self.block, self.one)
        elif n == 2:
            self.forward(self.base, self.block, self.one)
        elif n == 3:
            self.close(self.base, self.block, self.one)
            self.fan(self.base + 4, self.line, self.two)
        elif n == 4:
            self.forward(self.base + 4, self.line, self.two)
        else:
            self.close(self.base + 4, self.line, self.two)


OWN, OTHER = 0, 1
TO_OPPOSITE, TO_CROSS, TO_MATE, TO_OWN = 0, 1, 2, 3
UPPER, LOWER = slice(HALF, TOKENS), slice(0, HALF)


def block_kernel(
    length_ref, id_ref, x_ref, g_ref, wq_ref, wk_ref, wv_ref, qd_ref, vd_ref, qu_ref, vu_ref,
    grad_out, up_out, down_out,
    xs, ws, qds, vds, qus, vus, down, up, low, qkv, grads, cots, meta, dk_acc, dv_acc,
    sib_out, sib_in, ring_out, relay_in, ring_in, kept,
    low_mine, low_sib, low_chip, low_in, up_terms, down_terms,
    send_sems, recv_sems, local_sems,
):
    p = Place()
    net = Net(send_sems, recv_sems)
    copies = iter(range(32))

    def local(src, dst):
        copy = pltpu.make_async_copy(src, dst, local_sems.at[next(copies)])
        copy.start()
        return copy

    def cols_of(ref, start, width):
        return ref.at[..., pl.ds(pl.multiple_of(start, width), width)]

    def x_block(slot, flip, core, rows=slice(None)):
        column = pl.multiple_of(p.part(flip, core) * COLS, COLS)
        return xs.at[slot, rows, pl.ds(column, COLS)]

    my_rows = pl.ds(pl.multiple_of(p.z * ROWS, 32), ROWS)
    first = []
    for g in range(2):
        for ref, at, width in ((wq_ref, 0, 256), (wk_ref, 256, 128), (wv_ref, 384, 128)):
            c = g * GROUP + at
            first.append(
                local(
                    cols_of(ref, p.dp * 2 * width + g * width, width),
                    ws.at[p.y, my_rows, c : c + width],
                )
            )
    first.append(local(x_ref, x_block(OWN, 0, p.core)))
    later = [
        local(qd_ref, qds),
        local(vd_ref, vds),
        local(cols_of(qu_ref, p.dp * 512, 512), qus),
        local(cols_of(vu_ref, p.dp * 256, 256), vus),
        local(cols_of(g_ref, p.dp * 512, 512), cots.at[OWN]),
    ]
    line = lax.broadcasted_iota(jnp.int32, (8, 128), 0)
    meta[OWN] = jnp.where(line == 0, id_ref[0], length_ref[0])

    enter([
        p.mate, p.cross, p.opposite, p.sibling,
        p.ring_y(1), p.ring_y(-1), p.ring_z(1), p.ring_z(-1),
    ])

    net.send(0, meta.at[OWN], meta.at[OTHER], p.opposite)
    for copy in first:
        copy.wait()

    def weight_view(y, z, window):
        rows = slice(None) if z is None else pl.ds(pl.multiple_of(z * ROWS, 32), ROWS)
        return ws.at[slice(None) if y is None else y, rows, window]

    rounds = []
    for g in range(2):
        pair = []
        for h in range(2):
            c = g * GROUP + h * 256
            pair.append(
                TorusGather(
                    net, 32 + 8 * (2 * g + h), p, h == 0, weight_view,
                    slice(c, c + 256), slice(c, c + 128), slice(c + 128, c + 256),
                )
            )
        rounds.append(pair)

    def weights(g, stage):
        for one in rounds[g]:
            one.stage(stage)

    def x_send(index, slot, flip, rows, to_slot, device):
        net.send(
            index, x_block(slot, flip, p.core, rows), x_block(to_slot, flip, p.core, rows), device
        )

    weights(0, 1)
    weights(1, 1)
    every = slice(None)
    x_send(1, OWN, 0, UPPER, OWN, p.mate)
    x_send(2, OWN, 0, LOWER, OTHER, p.cross)
    x_send(3, OWN, 0, LOWER, OWN, p.mate)
    x_send(4, OWN, 0, UPPER, OTHER, p.cross)
    x_send(5, OWN, 0, every, OWN, p.sibling)
    weights(0, 2)
    weights(1, 2)
    weights(0, 3)

    for copy in later:
        copy.wait()
    net.arrived(0, meta.at[OTHER], p.opposite)
    up[...] = jnp.zeros_like(up)

    def choose(slot):
        chosen = meta[slot, 0:1, 0:1]

        def add(a, sums):
            weight = (chosen == a).astype(F32)
            return tuple(
                total + table[a].astype(F32) * weight
                for total, table in zip(sums, (qds, vds, qus, vus))
            )

        zeros = tuple(jnp.zeros((RANK, width), F32) for width in (D, D, 512, 256))
        q_rows, v_rows, q_up, v_up = lax.fori_loop(0, ADAPTERS, add, zeros)
        down[slot, :RANK, :] = q_rows.astype(BF16)
        down[slot, RANK:, :] = v_rows.astype(BF16)
        for g in range(2):
            c0 = g * GROUP
            up[slot, :RANK, c0 : c0 + 256] = q_up[:, g * 256 : g * 256 + 256].astype(BF16)
            up[slot, RANK:, c0 + 384 : c0 + 512] = v_up[:, g * 128 : g * 128 + 128].astype(BF16)

    choose(OWN)

    def x_arrived(index, slot, flip, rows, device, core=None):
        net.arrived(index, x_block(slot, flip, p.core if core is None else core, rows), device)

    x_arrived(1, OWN, 1, UPPER, p.mate)
    x_send(6, OWN, 1, UPPER, OTHER, p.cross)
    x_send(7, OWN, 1, UPPER, OWN, p.sibling)
    x_arrived(2, OTHER, 1, LOWER, p.cross)
    x_send(8, OTHER, 1, LOWER, OTHER, p.mate)
    x_send(9, OTHER, 1, LOWER, OTHER, p.sibling)
    for g in range(2):
        net.send(
            20 + g,
            cols_of(g_ref, (1 - p.dp) * 512 + g * 256, 256),
            cots.at[OTHER, :, g * 256 : g * 256 + 256],
            p.opposite,
        )
    choose(OTHER)
    weights(0, 4)
    weights(1, 3)
    x_arrived(3, OWN, 1, LOWER, p.mate)
    x_send(10, OWN, 1, LOWER, OWN, p.sibling)
    x_arrived(4, OTHER, 1, UPPER, p.cross)
    x_send(11, OTHER, 1, UPPER, OTHER, p.sibling)
    away = 1 - p.core
    x_arrived(5, OWN, 0, every, p.sibling, away)
    x_arrived(7, OWN, 1, UPPER, p.sibling, away)
    x_arrived(10, OWN, 1, LOWER, p.sibling, away)

    def rank_space(slot):
        low[slot] = dot(xs[slot], down[slot], ((1,), (1,))).astype(BF16)

    def project(slot, g):
        @pl.loop(0, 2)
        def _(n):
            window = pl.ds(pl.multiple_of(g * GROUP + n * 256, 256), 256)
            base = dot(xs[slot], ws[:, :, window].reshape(D, 256), ((1,), (0,)))
            extra = dot(low[slot], up[slot, :, window], ((1,), (0,)))
            qkv[slot, :, window] = (base + adapter_scale * extra).astype(BF16)

    def attend(slot, g, rows):
        c0 = g * GROUP
        start, step, span = rows.start, HALF, rows.stop
        length = meta[slot, 1:2, 0:1]
        k = qkv[slot, :span, c0 + 256 : c0 + 384]
        v = qkv[slot, :span, c0 + 384 : c0 + 512]
        key_at = lax.broadcasted_iota(jnp.int32, (span, step), 0)
        row_at = lax.broadcasted_iota(jnp.int32, (span, step), 1) + start
        allowed = (key_at <= row_at) & (key_at < length)
        used = lax.broadcasted_iota(jnp.int32, (step, HD), 0) + start < length
        dk, dv = 0.0, 0.0
        for h in range(2):
            q = qkv[slot, rows, c0 + h * HD : c0 + (h + 1) * HD]
            cot = cots[slot, rows, g * 256 + h * HD : g * 256 + (h + 1) * HD]
            cot = jnp.where(used, cot, jnp.zeros_like(cot))
            raw = dot(k, q, ((1,), (1,)))
            turned = jnp.tanh(raw * (score_scale / soft_cap))
            weight = jnp.where(allowed, jnp.exp(soft_cap * turned), 0.0)
            probs = weight * (1.0 / jnp.sum(weight, axis=0, keepdims=True))
            probs_b = probs.astype(BF16)
            dprob = dot(v, cot, ((1,), (1,)))
            row_total = jnp.sum(probs * dprob, axis=0, keepdims=True)
            dscore = (
                probs * (dprob - row_total) * ((1.0 - turned * turned) * score_scale)
            ).astype(BF16)
            dq = dot(k, dscore, ((0,), (0,)))
            grads[slot, rows, c0 + h * HD : c0 + (h + 1) * HD] = dq.T.astype(BF16)
            dk = dk + dot(dscore, q, ((1,), (0,)))
            dv = dv + dot(probs_b, cot, ((1,), (0,)))
        if rows.stop == TOKENS:
            dk_acc[...] = dk[:HALF]
            dv_acc[...] = dv[:HALF]
            dk, dv = dk[HALF:], dv[HALF:]
        else:
            dk, dv = dk + dk_acc[...], dv + dv_acc[...]
        grads[slot, rows, c0 + 256 : c0 + 384] = dk.astype(BF16)
        grads[slot, rows, c0 + 384 : c0 + 512] = dv.astype(BF16)

    rank_space(OWN)
    weights(0, 5)
    project(OWN, 0)
    attend(OWN, 0, UPPER)
    attend(OWN, 0, LOWER)

    x_arrived(6, OTHER, 0, UPPER, p.cross)
    x_send(12, OTHER, 0, UPPER, OTHER, p.sibling)
    x_arrived(8, OTHER, 0, LOWER, p.mate)
    x_send(13, OTHER, 0, LOWER, OTHER, p.sibling)
    weights(1, 4)
    x_arrived(9, OTHER, 1, LOWER, p.sibling, away)
    x_arrived(11, OTHER, 1, UPPER, p.sibling, away)
    x_arrived(12, OTHER, 0, UPPER, p.sibling, away)
    x_arrived(13, OTHER, 0, LOWER, p.sibling, away)
    rank_space(OTHER)
    project(OTHER, 0)
    net.arrived(20, cots.at[OTHER, :, 0:256], p.opposite)
    attend(OTHER, 0, UPPER)
    attend(OTHER, 0, LOWER)
    weights(1, 5)
    project(OTHER, 1)
    net.arrived(21, cots.at[OTHER, :, 256:512], p.opposite)
    attend(OTHER, 1, UPPER)

    slots = {TO_OPPOSITE: (OTHER, 0), TO_CROSS: (OTHER, 1), TO_MATE: (OWN, 1), TO_OWN: (OWN, 0)}
    chunk = 384

    def products(block, core, rows):
        slot, flip = slots[block]
        part = p.part(flip, core)
        for c in range(0, COLS, chunk):
            cols = slice(c, c + chunk)
            yield cols, dot(grads[slot, rows], ws[part, cols], ((1,), (1,)))

    def sib_index(block, rows):
        return 64 + 2 * block + (rows is UPPER)

    def for_sibling(block, rows):
        for cols, value in products(block, away, rows):
            sib_out[block, rows, cols] = value.astype(BF16)
        net.send(
            sib_index(block, rows), sib_out.at[block, rows], sib_in.at[block, rows], p.sibling
        )

    def both_cores(block, rows):
        net.arrived(sib_index(block, rows), sib_in.at[block, rows], p.sibling)
        for cols, value in products(block, p.core, rows):
            yield cols, value + sib_in[block, rows, cols].astype(F32)

    def to_ring(block, rows):
        for cols, value in both_cores(block, rows):
            ring_out[block, rows, cols] = value.astype(BF16)

    for_sibling(TO_OPPOSITE, UPPER)
    for_sibling(TO_CROSS, UPPER)
    to_ring(TO_OPPOSITE, UPPER)
    net.send(22, ring_out.at[TO_OPPOSITE, UPPER], relay_in.at[0], p.cross)
    to_ring(TO_CROSS, UPPER)
    net.send(24, ring_out.at[TO_CROSS, UPPER], ring_in.at[0, UPPER], p.cross)
    attend(OTHER, 1, LOWER)
    for_sibling(TO_OPPOSITE, LOWER)
    for_sibling(TO_CROSS, LOWER)
    to_ring(TO_OPPOSITE, LOWER)
    net.send(23, ring_out.at[TO_OPPOSITE, LOWER], relay_in.at[1], p.mate)
    project(OWN, 1)
    attend(OWN, 1, UPPER)
    attend(OWN, 1, LOWER)

    for slot in (OWN, OTHER):
        low_mine[slot] = adapter_scale * dot(up[slot], grads[slot], ((1,), (1,)))
    net.send(14, low_mine, low_sib, p.sibling)
    my_up = up_terms.at[p.dp, p.y, p.z]
    for slot in (OWN, OTHER):
        seq = p.dp if slot == OWN else 1 - p.dp
        terms = (adapter_scale * dot(low[slot], grads[slot], ((0,), (0,)))).astype(BF16)
        for g in range(2):
            c0 = g * GROUP
            at = pl.multiple_of(seq * 512 + g * 256, 256)
            my_up[:, pl.ds(at, 256)] = terms[:RANK, c0 : c0 + 256]
            at = pl.multiple_of(1024 + seq * 256 + g * 128, 128)
            my_up[:, pl.ds(at, 128)] = terms[RANK:, c0 + 384 : c0 + 512]
    my_up[:, 1536:UP] = jnp.broadcast_to(meta[OWN, 0:1, :], (RANK, 128)).astype(F32).astype(BF16)
    net.send(15, my_up, my_up, p.opposite)
    for_sibling(TO_MATE, LOWER)
    for_sibling(TO_MATE, UPPER)
    net.arrived(14, low_sib, p.sibling)
    low_chip[...] = low_mine[...] + low_sib[...]
    net.send(16, low_chip.at[OWN], low_in.at[0], p.mate)
    net.send(17, low_chip.at[OTHER], low_in.at[1], p.cross)
    net.send(18, low_chip.at[OTHER], low_in.at[2], p.opposite)
    to_ring(TO_MATE, LOWER)
    net.send(26, ring_out.at[TO_MATE, LOWER], ring_in.at[1, LOWER], p.mate)

    def terms_gather(base, ref, cuts):
        everything = slice(None)

        def view(y, z, window):
            return ref.at[
                :, everything if y is None else y, everything if z is None else z, :, window
            ]

        return [
            TorusGather(
                net, base + 8 * n, p, n == 0, view,
                slice(cuts[2 * n], cuts[2 * n + 2]),
                slice(cuts[2 * n], cuts[2 * n + 1]),
                slice(cuts[2 * n + 1], cuts[2 * n + 2]),
            )
            for n in range(2)
        ]

    up_gather = terms_gather(72, up_terms, (0, 384, 768, 1152, UP))
    down_gather = terms_gather(88, down_terms, (0, 640, 1152, 1792, DOWN))

    def stage(gather, n):
        for one in gather:
            one.stage(n)

    net.arrived(15, up_terms.at[1 - p.dp, p.y, p.z], p.opposite)
    stage(up_gather, 1)
    total = low_chip[OWN]
    for n, device in enumerate((p.mate, p.cross, p.opposite)):
        net.arrived(16 + n, low_in.at[n], device)
        total = total + low_in[n]
    low_grad = total.astype(BF16)
    my_cols = pl.ds(pl.multiple_of(p.t * COLS, COLS), COLS)
    my_x = x_block(OWN, 0, p.core)
    my_down = down_terms.at[p.dp, p.y, p.z]
    value = dot(low_grad, my_x[...], ((1,), (0,))).astype(BF16)
    my_down[:, 0:COLS] = value[:RANK]
    my_down[:, COLS:DOWN] = value[RANK:]
    net.send(19, my_down, my_down, p.opposite)

    for_sibling(TO_OWN, LOWER)
    for_sibling(TO_OWN, UPPER)
    to_ring(TO_MATE, UPPER)
    net.arrived(22, relay_in.at[0], p.cross)
    ring_out[TO_MATE, UPPER] = (
        ring_out[TO_MATE, UPPER].astype(F32) + relay_in[0].astype(F32)
    ).astype(BF16)
    net.send(27, ring_out.at[TO_MATE, UPPER], ring_in.at[1, UPPER], p.mate)
    stage(up_gather, 2)
    to_ring(TO_CROSS, LOWER)
    net.arrived(23, relay_in.at[1], p.mate)
    ring_out[TO_CROSS, LOWER] = (
        ring_out[TO_CROSS, LOWER].astype(F32) + relay_in[1].astype(F32)
    ).astype(BF16)
    net.send(25, ring_out.at[TO_CROSS, LOWER], ring_in.at[0, LOWER], p.cross)
    stage(up_gather, 3)
    net.arrived(19, down_terms.at[1 - p.dp, p.y, p.z], p.opposite)
    stage(down_gather, 1)
    for rows in (LOWER, UPPER):
        for cols, value in both_cores(TO_OWN, rows):
            kept[rows, cols] = value
    kept[...] += dot(low_grad, down[OWN, :, my_cols], ((0,), (0,)))
    stage(up_gather, 4)
    stage(down_gather, 2)
    stage(down_gather, 3)
    stage(up_gather, 5)
    save_up = local(up_terms, up_out)
    stage(down_gather, 4)
    for index, n, rows, device in (
        (24, 0, UPPER, p.cross), (26, 1, LOWER, p.mate),
        (27, 1, UPPER, p.mate), (25, 0, LOWER, p.cross),
    ):
        net.arrived(index, ring_in.at[n, rows], device)
    grad_out[...] = (
        kept[...] + ring_in[0].astype(F32) + ring_in[1].astype(F32)
    ).astype(BF16)
    stage(down_gather, 5)
    save_down = local(down_terms, down_out)
    net.finish()
    save_up.wait()
    save_down.wait()


def block_call(lengths, ids, *arrays):
    hbm = pl.BlockSpec(memory_space=pl.ANY)
    vmem = pl.BlockSpec(memory_space=pltpu.VMEM)
    smem = pl.BlockSpec(memory_space=pltpu.SMEM)
    bf16 = lambda *shape: pltpu.VMEM(shape, BF16)
    f32 = lambda *shape: pltpu.VMEM(shape, F32)
    return pl.pallas_call(
        block_kernel,
        name="attention_block",
        out_shape=(
            jax.ShapeDtypeStruct((TOKENS, COLS), BF16),
            jax.ShapeDtypeStruct((2, SIDE, SIDE, RANK, UP), BF16),
            jax.ShapeDtypeStruct((2, SIDE, SIDE, RANK, DOWN), BF16),
        ),
        in_specs=[smem, smem] + [hbm] * 9,
        out_specs=(vmem, hbm, hbm),
        scratch_shapes=[
            bf16(2, TOKENS, D),
            bf16(SIDE, COLS, 2 * GROUP),
            bf16(ADAPTERS, RANK, D),
            bf16(ADAPTERS, RANK, D),
            bf16(ADAPTERS, RANK, 512),
            bf16(ADAPTERS, RANK, 256),
            bf16(2, 2 * RANK, D),
            bf16(2, 2 * RANK, 2 * GROUP),
            bf16(2, TOKENS, 2 * RANK),
            bf16(2, TOKENS, 2 * GROUP),
            bf16(2, TOKENS, 2 * GROUP),
            bf16(2, TOKENS, 512),
            pltpu.VMEM((2, 8, 128), jnp.int32),
            f32(HALF, HD),
            f32(HALF, HD),
            bf16(4, TOKENS, COLS),
            bf16(4, TOKENS, COLS),
            bf16(3, TOKENS, COLS),
            bf16(2, HALF, COLS),
            bf16(2, TOKENS, COLS),
            f32(TOKENS, COLS),
            f32(2, 2 * RANK, TOKENS),
            f32(2, 2 * RANK, TOKENS),
            f32(2, 2 * RANK, TOKENS),
            f32(3, 2 * RANK, TOKENS),
            bf16(2, SIDE, SIDE, RANK, UP),
            bf16(2, SIDE, SIDE, RANK, DOWN),
            pltpu.SemaphoreType.DMA((104,)),
            pltpu.SemaphoreType.DMA((104,)),
            pltpu.SemaphoreType.DMA((14,)),
        ],
        compiler_params=pltpu.CompilerParams(
            collective_id=0, has_side_effects=True, vmem_limit_bytes=VMEM_BYTES
        ),
    )(lengths, ids, *arrays)


def table_kernel(grad_ref, up_ref, down_ref, grad_out, qa_out, qb_out, va_out, vb_out, sem):
    copy = pltpu.make_async_copy(grad_ref, grad_out, sem)
    copy.start()
    rows = 16 * RANK
    at = lax.broadcasted_iota(jnp.int32, (rows, rows), 0)
    to = lax.broadcasted_iota(jnp.int32, (rows, rows), 1)
    owners = []
    for s in range(2):
        chosen = up_ref[s, :, 1536:1537].astype(F32)
        own = ((to // RANK).astype(F32) == chosen) & (at % RANK == to % RANK)
        owners.append(own.astype(F32).T.astype(BF16))

    def total(first, second):
        return dot(owners[0], first, ((1,), (0,))) + dot(owners[1], second, ((1,), (0,)))

    for c in range(0, COLS, 384):
        cols = slice(c, c + 384)
        qa_out[:, cols] = total(down_ref[0, :, cols], down_ref[1, :, cols])
        cols = slice(COLS + c, COLS + c + 384)
        va_out[:, c : c + 384] = total(down_ref[0, :, cols], down_ref[1, :, cols])
    for d in range(2):
        for out, start, width in ((qb_out, 0, 512), (vb_out, 1024, 256)):
            out[:, d * width : (d + 1) * width] = total(
                up_ref[d, :, start : start + width],
                up_ref[d, :, start + width : start + 2 * width],
            )
    copy.wait()


def table_call(grad, up_terms, down_terms):
    hbm = pl.BlockSpec(memory_space=pl.ANY)
    vmem = pl.BlockSpec(memory_space=pltpu.VMEM)
    rows = 16 * RANK
    table = lambda width: jax.ShapeDtypeStruct((rows, width), F32)
    return pl.pallas_call(
        table_kernel,
        name="tables",
        out_shape=(
            jax.ShapeDtypeStruct((TOKENS, COLS), BF16),
            table(COLS), table(1024), table(COLS), table(512),
        ),
        in_specs=[hbm, vmem, vmem],
        out_specs=(hbm, vmem, vmem, vmem, vmem),
        scratch_shapes=[pltpu.SemaphoreType.DMA],
        compiler_params=pltpu.CompilerParams(vmem_limit_bytes=VMEM_BYTES),
    )(grad, up_terms.reshape(2, rows, UP), down_terms.reshape(2, rows, DOWN))


def shards(
    x_in, lengths, adapter_ids, attn_grad, w_query, w_key, w_value,
    query_down, query_up, value_down, value_up,
):
    grad, up_terms, down_terms = block_call(
        lengths, adapter_ids, x_in[0], attn_grad[0], w_query, w_key, w_value,
        query_down, value_down, query_up, value_up,
    )
    grad, qa, qb, va, vb = table_call(grad, up_terms, down_terms)
    tables = (table.reshape(ADAPTERS, RANK, -1) for table in (qa, qb, va, vb))
    return (grad[None], *tables)


def solution(mesh):
    placed = (
        P(("dp", "fsdp"), None, "tensor"),
        P(("dp", "fsdp")),
        P(("dp", "fsdp")),
        P(("dp", "fsdp"), None, "tensor"),
        P("fsdp", "tensor"),
        P("fsdp", "tensor"),
        P("fsdp", "tensor"),
        P(),
        P(None, None, "tensor"),
        P(),
        P(None, None, "tensor"),
    )
    return jax.shard_map(
        shards,
        mesh=mesh,
        in_specs=placed,
        out_specs=(
            P(("dp", "fsdp"), None, "tensor"),
            P(None, None, "tensor"),
            P(None, None, "tensor"),
            P(None, None, "tensor"),
            P(None, None, "tensor"),
        ),
        check_vma=False,
    )
```

time: 805 us -> 180 us (0.22)
  waiting for transfers between devices: 644 us -> 0 us
  Pallas kernels: 0 us -> 178 us
  matrix products: 114 us -> 0 us
  local copies, waits for them, and re-layouts: 14.4 us -> 0 us
  between operations: 15.6 us -> 2.11 us
  blocking collectives: 12.5 us -> 0 us
    psum x1 -> x0, waiting for transfers between devices: 365 us -> none  [shards(): lax.psum((owner_row[:, None, None] * term_qa[None], owner_row[:, None, No...]
    all_gather x4 -> x0, waiting for transfers between devices: 207 us -> none  [the longest x1 70.9 us: shards(): lax.all_gather(w_query, 'fsdp', axis=0, tiled=True)]
    pallas_call x0 -> x2, Pallas kernels: none -> 178 us  [the longest x1 137 us: block_call(): pl.pallas_call(block_kernel, name='attention_block', out_shape=(jax.Shape...]
    dot_general x27 -> x0, matrix products: 114 us -> none  [the longest x5 25.6 us: flipped_matrix_product(): lax.dot_general(left, right, (((1,), (1,)), ((), ())), preferred_element_...]
    reduce_scatter x1 -> x0, waiting for transfers between devices: 69.5 us -> none  [shards(): lax.psum_scatter(partial_value, 'tensor', scatter_dimension=1, tiled=True)]
    psum x1 -> x0, blocking collectives: 12.5 us -> none  [shards(): sum_q, sum_v = lax.psum((query_portion, value_portion), 'tensor')]
    unnamed x28 -> x0, local copies, waits for them, and re-layouts: 12.3 us -> none
  transfers between devices with their start and end apart: 6 -> 0, of which waited for: 6 -> 0; matrix products, arithmetic and copies ran while one was open for 6% -> 0% of each run, Pallas kernels for 0% -> 0%
where the time goes in v3:
time: 180 us
  Pallas kernels  178 us (99%)
  between operations  2.11 us (1%)
    pallas_call x1, Pallas kernels, block_call(): pl.pallas_call(block_kernel, name='attention_block', out_shape=(jax.Shape...  137 us
    pallas_call x1, Pallas kernels, table_call(): pl.pallas_call(table_kernel, name='tables', out_shape=(jax.ShapeDtypeStru...  40.9 us

profile of v3, /device:TPU:0, one launch (start us, length us, event | category | flops | bytes accessed | tf_op | source)
XLA Modules:
  0.0 180.1 jit_solution(11138699420530613400)
XLA Ops:
  1.9 137.0 %attention_block.1 = (bf16[512,1152]{1,0:T(8,128)(2,1)}, bf16[2,4,4,16,1664]{4,3,2,1,0:T(8,128)(2,1)}, bf16[2,4,4,16,2304]{4,3,2,1,0:T(8,128)(2,1)}) custom-call(s32[1]{0:T(128)S(6)} %copy.16.length_ref, s32[1]{0:T(128)S(6)} %copy.17.id_ref, bf16[512,1152]{1,0:T(8,128)(2,1)} %bitcast.11, bf16[512,1024]{1,0:T(8,128)(2,1)} %bitcast.12, ...), custom_call_target="tpu_custom_call" | custom-call | tf_op jit(solution)/shard_map/attention_block/pallas_call | solution.py:531
  139.0 40.9 %tables.1 = (bf16[512,1152]{1,0:T(8,128)(2,1)}, f32[256,1152]{1,0:T(8,128)}, f32[256,1024]{1,0:T(8,128)}, f32[256,1152]{1,0:T(8,128)}, f32[256,512]{1,0:T(8,128)}) custom-call(bf16[512,1152]{1,0:T(8,128)(2,1)} %get-tuple-element.13.grad_ref, bf16[2,256,1664]{2,1,0:T(8,128)(2,1)} %bitcast.10, bf16[2,256,2304]{2,1,0:T(8,128)(2,1)} %bitcast.9), custom_call_target="tpu_custom_call" | custom-call | tf_op jit(solution)/shard_map/tables/pallas_call | solution.py:613

commit v4 on v3

--- a/solution.py
+++ b/solution.py
@@ -403,8 +403,6 @@
     for_sibling(TO_CROSS, UPPER)
     to_ring(TO_OPPOSITE, UPPER)
     net.send(22, ring_out.at[TO_OPPOSITE, UPPER], relay_in.at[0], p.cross)
-    to_ring(TO_CROSS, UPPER)
-    net.send(24, ring_out.at[TO_CROSS, UPPER], ring_in.at[0, UPPER], p.cross)
     attend(OTHER, 1, LOWER)
     for_sibling(TO_OPPOSITE, LOWER)
     for_sibling(TO_CROSS, LOWER)
@@ -429,13 +427,15 @@
             my_up[:, pl.ds(at, 128)] = terms[RANK:, c0 + 384 : c0 + 512]
     my_up[:, 1536:UP] = jnp.broadcast_to(meta[OWN, 0:1, :], (RANK, 128)).astype(F32).astype(BF16)
     net.send(15, my_up, my_up, p.opposite)
+    to_ring(TO_CROSS, UPPER)
+    net.arrived(14, low_sib, p.sibling)
+    low_chip[...] = (low_mine[...] + low_sib[...]).astype(BF16)
+    net.send(16, low_chip, low_in.at[0], p.mate)
+    net.send(17, low_chip, low_in.at[1], p.cross)
+    net.send(18, low_chip, low_in.at[2], p.opposite)
+    net.send(24, ring_out.at[TO_CROSS, UPPER], ring_in.at[0, UPPER], p.cross)
     for_sibling(TO_MATE, LOWER)
     for_sibling(TO_MATE, UPPER)
-    net.arrived(14, low_sib, p.sibling)
-    low_chip[...] = low_mine[...] + low_sib[...]
-    net.send(16, low_chip.at[OWN], low_in.at[0], p.mate)
-    net.send(17, low_chip.at[OTHER], low_in.at[1], p.cross)
-    net.send(18, low_chip.at[OTHER], low_in.at[2], p.opposite)
     to_ring(TO_MATE, LOWER)
     net.send(26, ring_out.at[TO_MATE, LOWER], ring_in.at[1, LOWER], p.mate)
 
@@ -466,19 +466,6 @@
 
     net.arrived(15, up_terms.at[1 - p.dp, p.y, p.z], p.opposite)
     stage(up_gather, 1)
-    total = low_chip[OWN]
-    for n, device in enumerate((p.mate, p.cross, p.opposite)):
-        net.arrived(16 + n, low_in.at[n], device)
-        total = total + low_in[n]
-    low_grad = total.astype(BF16)
-    my_cols = pl.ds(pl.multiple_of(p.t * COLS, COLS), COLS)
-    my_x = x_block(OWN, 0, p.core)
-    my_down = down_terms.at[p.dp, p.y, p.z]
-    value = dot(low_grad, my_x[...], ((1,), (0,))).astype(BF16)
-    my_down[:, 0:COLS] = value[:RANK]
-    my_down[:, COLS:DOWN] = value[RANK:]
-    net.send(19, my_down, my_down, p.opposite)
-
     for_sibling(TO_OWN, LOWER)
     for_sibling(TO_OWN, UPPER)
     to_ring(TO_MATE, UPPER)
@@ -488,6 +475,20 @@
     ).astype(BF16)
     net.send(27, ring_out.at[TO_MATE, UPPER], ring_in.at[1, UPPER], p.mate)
     stage(up_gather, 2)
+
+    for n, device in enumerate((p.mate, p.cross, p.opposite)):
+        net.arrived(16 + n, low_in.at[n], device)
+    my_cols = pl.ds(pl.multiple_of(p.t * COLS, COLS), COLS)
+    low_grads = []
+    for slot in (OWN, OTHER):
+        pair = low_chip[slot].astype(F32) + low_in[0, slot].astype(F32)
+        far = low_in[1, 1 - slot].astype(F32) + low_in[2, 1 - slot].astype(F32)
+        low_grads.append((pair + far).astype(BF16))
+        value = dot(low_grads[slot], xs[slot, :, my_cols], ((1,), (0,))).astype(BF16)
+        my_down = down_terms.at[p.dp if slot == OWN else 1 - p.dp, p.y, p.z]
+        my_down[:, 0:COLS] = value[:RANK]
+        my_down[:, COLS:DOWN] = value[RANK:]
+    stage(down_gather, 1)
     to_ring(TO_CROSS, LOWER)
     net.arrived(23, relay_in.at[1], p.mate)
     ring_out[TO_CROSS, LOWER] = (
@@ -495,18 +496,18 @@
     ).astype(BF16)
     net.send(25, ring_out.at[TO_CROSS, LOWER], ring_in.at[0, LOWER], p.cross)
     stage(up_gather, 3)
-    net.arrived(19, down_terms.at[1 - p.dp, p.y, p.z], p.opposite)
-    stage(down_gather, 1)
+    stage(down_gather, 2)
     for rows in (LOWER, UPPER):
         for cols, value in both_cores(TO_OWN, rows):
             kept[rows, cols] = value
-    kept[...] += dot(low_grad, down[OWN, :, my_cols], ((0,), (0,)))
+    kept[...] += dot(low_grads[OWN], down[OWN, :, my_cols], ((0,), (0,)))
+    stage(down_gather, 3)
     stage(up_gather, 4)
-    stage(down_gather, 2)
-    stage(down_gather, 3)
     stage(up_gather, 5)
     save_up = local(up_terms, up_out)
     stage(down_gather, 4)
+    stage(down_gather, 5)
+    save_down = local(down_terms, down_out)
     for index, n, rows, device in (
         (24, 0, UPPER, p.cross), (26, 1, LOWER, p.mate),
         (27, 1, UPPER, p.mate), (25, 0, LOWER, p.cross),
@@ -515,8 +516,6 @@
     grad_out[...] = (
         kept[...] + ring_in[0].astype(F32) + ring_in[1].astype(F32)
     ).astype(BF16)
-    stage(down_gather, 5)
-    save_down = local(down_terms, down_out)
     net.finish()
     save_up.wait()
     save_down.wait()
@@ -562,8 +561,8 @@
             f32(TOKENS, COLS),
             f32(2, 2 * RANK, TOKENS),
             f32(2, 2 * RANK, TOKENS),
-            f32(2, 2 * RANK, TOKENS),
-            f32(3, 2 * RANK, TOKENS),
+            bf16(2, 2 * RANK, TOKENS),
+            bf16(3, 2, 2 * RANK, TOKENS),
             bf16(2, SIDE, SIDE, RANK, UP),
             bf16(2, SIDE, SIDE, RANK, DOWN),
             pltpu.SemaphoreType.DMA((104,)),
@@ -576,9 +575,8 @@
     )(lengths, ids, *arrays)
 
 
-def table_kernel(grad_ref, up_ref, down_ref, grad_out, qa_out, qb_out, va_out, vb_out, sem):
-    copy = pltpu.make_async_copy(grad_ref, grad_out, sem)
-    copy.start()
+def table_kernel(grad_ref, up_ref, down_ref, grad_out, qa_out, qb_out, va_out, vb_out):
+    grad_out[...] = grad_ref[...]
     rows = 16 * RANK
     at = lax.broadcasted_iota(jnp.int32, (rows, rows), 0)
     to = lax.broadcasted_iota(jnp.int32, (rows, rows), 1)
@@ -602,11 +600,9 @@
                 up_ref[d, :, start : start + width],
                 up_ref[d, :, start + width : start + 2 * width],
             )
-    copy.wait()
 
 
 def table_call(grad, up_terms, down_terms):
-    hbm = pl.BlockSpec(memory_space=pl.ANY)
     vmem = pl.BlockSpec(memory_space=pltpu.VMEM)
     rows = 16 * RANK
     table = lambda width: jax.ShapeDtypeStruct((rows, width), F32)
@@ -617,9 +613,8 @@
             jax.ShapeDtypeStruct((TOKENS, COLS), BF16),
             table(COLS), table(1024), table(COLS), table(512),
         ),
-        in_specs=[hbm, vmem, vmem],
-        out_specs=(hbm, vmem, vmem, vmem, vmem),
-        scratch_shapes=[pltpu.SemaphoreType.DMA],
+        in_specs=[vmem, vmem, vmem],
+        out_specs=(vmem, vmem, vmem, vmem, vmem),
         compiler_params=pltpu.CompilerParams(vmem_limit_bytes=VMEM_BYTES),
     )(grad, up_terms.reshape(2, rows, UP), down_terms.reshape(2, rows, DOWN))
 

time: 180 us -> 132 us (0.73)
  Pallas kernels: 178 us -> 129 us
    pallas_call x1, Pallas kernels: 40.9 us -> 5.83 us  [table_call(): pl.pallas_call(table_kernel, name='tables', out_shape=(jax.ShapeDtypeStru...]
    pallas_call x1, Pallas kernels: 137 us -> 124 us  [block_call(): pl.pallas_call(block_kernel, name='attention_block', out_shape=(jax.Shape...]
where the time goes in v4:
time: 132 us; the launch traced here: 131 us
  Pallas kernels  129 us (98%)
  between operations  1.93 us (1%)
    pallas_call x1, Pallas kernels, block_call(): pl.pallas_call(block_kernel, name='attention_block', out_shape=(jax.Shape...  124 us
    pallas_call x1, Pallas kernels, table_call(): pl.pallas_call(table_kernel, name='tables', out_shape=(jax.ShapeDtypeStru...  5.83 us

profile of v4, /device:TPU:0, one launch (start us, length us, event | category | flops | bytes accessed | tf_op | source)
XLA Modules:
  0.0 131.3 jit_solution(7763195378998011377)
XLA Ops:
  1.9 123.6 %attention_block.1 = (bf16[512,1152]{1,0:T(8,128)(2,1)}, bf16[2,4,4,16,1664]{4,3,2,1,0:T(8,128)(2,1)}, bf16[2,4,4,16,2304]{4,3,2,1,0:T(8,128)(2,1)}) custom-call(s32[1]{0:T(128)S(6)} %copy.16.length_ref, s32[1]{0:T(128)S(6)} %copy.17.id_ref, bf16[512,1152]{1,0:T(8,128)(2,1)} %bitcast.11, bf16[512,1024]{1,0:T(8,128)(2,1)} %bitcast.12, ...), custom_call_target="tpu_custom_call" | custom-call | tf_op jit(solution)/shard_map/attention_block/pallas_call | solution.py:530
  125.5 5.8 %tables.1 = (bf16[512,1152]{1,0:T(8,128)(2,1)}, f32[256,1152]{1,0:T(8,128)}, f32[256,1024]{1,0:T(8,128)}, f32[256,1152]{1,0:T(8,128)}, f32[256,512]{1,0:T(8,128)}) custom-call(bf16[512,1152]{1,0:T(8,128)(2,1)} %get-tuple-element.13.grad_ref, bf16[2,256,1664]{2,1,0:T(8,128)(2,1)} %bitcast.10, bf16[2,256,2304]{2,1,0:T(8,128)(2,1)} %bitcast.9), custom_call_target="tpu_custom_call" | custom-call | tf_op jit(solution)/shard_map/tables/pallas_call | solution.py:609

commit v5 on v4

--- a/solution.py
+++ b/solution.py
@@ -100,9 +100,9 @@
 
 
 class TorusGather:
-    def __init__(self, net, base, place, y_first, view, whole, low, high):
+    def __init__(self, net, base, place, y_first, view, low, high):
         self.net, self.base = net, base
-        self.whole, self.low, self.high = whole, low, high
+        self.low, self.high = low, high
         p = place
         if y_first:
             self.one, self.two = p.ring_y, p.ring_z
@@ -114,21 +114,25 @@
             self.line = lambda n, w: view((p.y + n) % SIDE, None, w)
 
     def fan(self, base, region, ring):
-        own = region(0, self.whole)
-        self.net.send(base, own, own, ring(1))
-        self.net.send(base + 1, own, own, ring(-1))
+        low, high = region(0, self.low), region(0, self.high)
+        self.net.send(base, low, low, ring(1))
+        self.net.send(base + 1, high, high, ring(-1))
+        self.net.send(base + 2, high, high, ring(1))
+        self.net.send(base + 3, low, low, ring(-1))
 
     def forward(self, base, region, ring):
-        self.net.arrived(base, region(-1, self.whole), ring(-1))
         part = region(-1, self.low)
-        self.net.send(base + 2, part, part, ring(1))
-        self.net.arrived(base + 1, region(1, self.whole), ring(1))
+        self.net.arrived(base, part, ring(-1))
+        self.net.send(base + 4, part, part, ring(1))
         part = region(1, self.high)
-        self.net.send(base + 3, part, part, ring(-1))
+        self.net.arrived(base + 1, part, ring(1))
+        self.net.send(base + 5, part, part, ring(-1))
 
     def close(self, base, region, ring):
-        self.net.arrived(base + 2, region(2, self.low), ring(-1))
-        self.net.arrived(base + 3, region(2, self.high), ring(1))
+        self.net.arrived(base + 2, region(-1, self.high), ring(-1))
+        self.net.arrived(base + 3, region(1, self.low), ring(1))
+        self.net.arrived(base + 4, region(2, self.low), ring(-1))
+        self.net.arrived(base + 5, region(2, self.high), ring(1))
 
     def stage(self, n):
         if n == 1:
@@ -137,11 +141,11 @@
             self.forward(self.base, self.block, self.one)
         elif n == 3:
             self.close(self.base, self.block, self.one)
-            self.fan(self.base + 4, self.line, self.two)
+            self.fan(self.base + 6, self.line, self.two)
         elif n == 4:
-            self.forward(self.base + 4, self.line, self.two)
+            self.forward(self.base + 6, self.line, self.two)
         else:
-            self.close(self.base + 4, self.line, self.two)
+            self.close(self.base + 6, self.line, self.two)
 
 
 OWN, OTHER = 0, 1
@@ -154,7 +158,7 @@
     grad_out, up_out, down_out,
     xs, ws, qds, vds, qus, vus, down, up, low, qkv, grads, cots, meta, dk_acc, dv_acc,
     sib_out, sib_in, ring_out, relay_in, ring_in, kept,
-    low_mine, low_sib, low_chip, low_in, up_terms, down_terms,
+    low_mine, low_sib, low_chip, low_in, low_grad, up_terms, down_terms, low_acc, proj_acc,
     send_sems, recv_sems, local_sems,
 ):
     p = Place()
@@ -174,7 +178,7 @@
         return xs.at[slot, rows, pl.ds(column, COLS)]
 
     my_rows = pl.ds(pl.multiple_of(p.z * ROWS, 32), ROWS)
-    first = []
+    first = [local(x_ref, x_block(OWN, 0, p.core))]
     for g in range(2):
         for ref, at, width in ((wq_ref, 0, 256), (wk_ref, 256, 128), (wv_ref, 384, 128)):
             c = g * GROUP + at
@@ -184,7 +188,6 @@
                     ws.at[p.y, my_rows, c : c + width],
                 )
             )
-    first.append(local(x_ref, x_block(OWN, 0, p.core)))
     later = [
         local(qd_ref, qds),
         local(vd_ref, vds),
@@ -201,8 +204,6 @@
     ])
 
     net.send(0, meta.at[OWN], meta.at[OTHER], p.opposite)
-    for copy in first:
-        copy.wait()
 
     def weight_view(y, z, window):
         rows = slice(None) if z is None else pl.ds(pl.multiple_of(z * ROWS, 32), ROWS)
@@ -215,8 +216,8 @@
             c = g * GROUP + h * 256
             pair.append(
                 TorusGather(
-                    net, 32 + 8 * (2 * g + h), p, h == 0, weight_view,
-                    slice(c, c + 256), slice(c, c + 128), slice(c + 128, c + 256),
+                    net, 40 + 12 * (2 * g + h), p, h == 0, weight_view,
+                    slice(c, c + 128), slice(c + 128, c + 256),
                 )
             )
         rounds.append(pair)
@@ -230,14 +231,25 @@
             index, x_block(slot, flip, p.core, rows), x_block(to_slot, flip, p.core, rows), device
         )
 
+    for copy in first:
+        copy.wait()
     weights(0, 1)
     weights(1, 1)
     every = slice(None)
-    x_send(1, OWN, 0, UPPER, OWN, p.mate)
-    x_send(2, OWN, 0, LOWER, OTHER, p.cross)
-    x_send(3, OWN, 0, LOWER, OWN, p.mate)
-    x_send(4, OWN, 0, UPPER, OTHER, p.cross)
-    x_send(5, OWN, 0, every, OWN, p.sibling)
+    for index, rows, to_slot, device in (
+        (1, UPPER, OWN, p.mate), (2, LOWER, OTHER, p.cross),
+        (3, LOWER, OWN, p.mate), (4, UPPER, OTHER, p.cross), (5, every, OWN, p.sibling),
+    ):
+        net.send(index, x_block(OWN, 0, p.core, rows), x_block(to_slot, 0, p.core, rows), device)
+
+    def send_cotangent(index, rows):
+        net.send(
+            index,
+            g_ref.at[rows, pl.ds(pl.multiple_of((1 - p.dp) * 512, 512), 512)],
+            cots.at[OTHER, rows],
+            p.opposite,
+        )
+
     weights(0, 2)
     weights(1, 2)
     weights(0, 3)
@@ -277,13 +289,8 @@
     x_arrived(2, OTHER, 1, LOWER, p.cross)
     x_send(8, OTHER, 1, LOWER, OTHER, p.mate)
     x_send(9, OTHER, 1, LOWER, OTHER, p.sibling)
-    for g in range(2):
-        net.send(
-            20 + g,
-            cols_of(g_ref, (1 - p.dp) * 512 + g * 256, 256),
-            cots.at[OTHER, :, g * 256 : g * 256 + 256],
-            p.opposite,
-        )
+    send_cotangent(20, UPPER)
+    send_cotangent(21, LOWER)
     choose(OTHER)
     weights(0, 4)
     weights(1, 3)
@@ -337,11 +344,11 @@
             dk = dk + dot(dscore, q, ((1,), (0,)))
             dv = dv + dot(probs_b, cot, ((1,), (0,)))
         if rows.stop == TOKENS:
-            dk_acc[...] = dk[:HALF]
-            dv_acc[...] = dv[:HALF]
+            dk_acc[g] = dk[:HALF]
+            dv_acc[g] = dv[:HALF]
             dk, dv = dk[HALF:], dv[HALF:]
         else:
-            dk, dv = dk + dk_acc[...], dv + dv_acc[...]
+            dk, dv = dk + dk_acc[g], dv + dv_acc[g]
         grads[slot, rows, c0 + 256 : c0 + 384] = dk.astype(BF16)
         grads[slot, rows, c0 + 384 : c0 + 512] = dv.astype(BF16)
 
@@ -351,63 +358,116 @@
     attend(OWN, 0, UPPER)
     attend(OWN, 0, LOWER)
 
+    x_arrived(9, OTHER, 1, LOWER, p.sibling, away)
+    x_arrived(11, OTHER, 1, UPPER, p.sibling, away)
+    wide = 2 * COLS
+
+    def half_of(flip):
+        lo = (p.x_lo + flip) % 2
+        return pl.ds(pl.multiple_of(lo * wide, wide), wide), pl.ds(lo * 2, 2)
+
+    columns, parts = half_of(1)
+    low_acc[...] = dot(xs[OTHER, :, columns], down[OTHER, :, columns], ((1,), (1,)))
+
+    @pl.loop(0, 2)
+    def _(n):
+        window = pl.ds(pl.multiple_of(n * 256, 256), 256)
+        proj_acc[:, window] = dot(
+            xs[OTHER, :, columns], ws[parts, :, window].reshape(wide, 256), ((1,), (0,))
+        )
+
     x_arrived(6, OTHER, 0, UPPER, p.cross)
     x_send(12, OTHER, 0, UPPER, OTHER, p.sibling)
     x_arrived(8, OTHER, 0, LOWER, p.mate)
     x_send(13, OTHER, 0, LOWER, OTHER, p.sibling)
     weights(1, 4)
-    x_arrived(9, OTHER, 1, LOWER, p.sibling, away)
-    x_arrived(11, OTHER, 1, UPPER, p.sibling, away)
     x_arrived(12, OTHER, 0, UPPER, p.sibling, away)
     x_arrived(13, OTHER, 0, LOWER, p.sibling, away)
-    rank_space(OTHER)
-    project(OTHER, 0)
-    net.arrived(20, cots.at[OTHER, :, 0:256], p.opposite)
+    columns, parts = half_of(0)
+    rest = dot(xs[OTHER, :, columns], down[OTHER, :, columns], ((1,), (1,)))
+    low[OTHER] = (low_acc[...] + rest).astype(BF16)
+
+    @pl.loop(0, 2)
+    def _(n):
+        window = pl.ds(pl.multiple_of(n * 256, 256), 256)
+        base = dot(xs[OTHER, :, columns], ws[parts, :, window].reshape(wide, 256), ((1,), (0,)))
+        extra = dot(low[OTHER], up[OTHER, :, window], ((1,), (0,)))
+        qkv[OTHER, :, window] = (
+            base + proj_acc[:, window] + adapter_scale * extra
+        ).astype(BF16)
+
+    net.arrived(20, cots.at[OTHER, UPPER], p.opposite)
     attend(OTHER, 0, UPPER)
-    attend(OTHER, 0, LOWER)
     weights(1, 5)
     project(OTHER, 1)
-    net.arrived(21, cots.at[OTHER, :, 256:512], p.opposite)
     attend(OTHER, 1, UPPER)
 
     slots = {TO_OPPOSITE: (OTHER, 0), TO_CROSS: (OTHER, 1), TO_MATE: (OWN, 1), TO_OWN: (OWN, 0)}
-    chunk = 384
-
-    def products(block, core, rows):
+
+    def piece(rows, side):
+        cut = 640 if rows is UPPER else 512
+        return slice(0, cut) if side == 0 else slice(cut, COLS)
+
+    def product(block, core, rows, cols):
         slot, flip = slots[block]
-        part = p.part(flip, core)
-        for c in range(0, COLS, chunk):
-            cols = slice(c, c + chunk)
-            yield cols, dot(grads[slot, rows], ws[part, cols], ((1,), (1,)))
-
-    def sib_index(block, rows):
-        return 64 + 2 * block + (rows is UPPER)
+        return dot(grads[slot, rows], ws[p.part(flip, core), cols], ((1,), (1,)))
+
+    def sib_index(block, rows, side):
+        return 136 + 4 * block + 2 * (rows is UPPER) + side
 
     def for_sibling(block, rows):
-        for cols, value in products(block, away, rows):
-            sib_out[block, rows, cols] = value.astype(BF16)
-        net.send(
-            sib_index(block, rows), sib_out.at[block, rows], sib_in.at[block, rows], p.sibling
+        for side in range(2):
+            cols = piece(rows, side)
+            sib_out[block, rows, cols] = product(block, away, rows, cols).astype(BF16)
+            net.send(
+                sib_index(block, rows, side),
+                sib_out.at[block, rows, cols], sib_in.at[block, rows, cols], p.sibling,
+            )
+
+    def both_cores(block, rows, side):
+        cols = piece(rows, side)
+        value = product(block, p.core, rows, cols)
+        net.arrived(sib_index(block, rows, side), sib_in.at[block, rows, cols], p.sibling)
+        return value + sib_in[block, rows, cols].astype(F32)
+
+    def ring_index(block, rows, side):
+        return 20 + 4 * block + 2 * (rows is UPPER) + side if block else (
+            32 + 2 * (rows is UPPER) + side
         )
 
-    def both_cores(block, rows):
-        net.arrived(sib_index(block, rows), sib_in.at[block, rows], p.sibling)
-        for cols, value in products(block, p.core, rows):
-            yield cols, value + sib_in[block, rows, cols].astype(F32)
-
-    def to_ring(block, rows):
-        for cols, value in both_cores(block, rows):
-            ring_out[block, rows, cols] = value.astype(BF16)
+    def to_ring(block, rows, side, relay=None):
+        cols = piece(rows, side)
+        value = both_cores(block, rows, side)
+        if relay is not None:
+            net.arrived(
+                ring_index(TO_OPPOSITE, rows, side), relay_in.at[rows, cols],
+                (p.cross, p.mate)[side],
+            )
+            value = value + relay_in[rows, cols].astype(F32)
+        ring_out[block, rows, cols] = value.astype(BF16)
+
+    def ship(block, rows, side):
+        cols = piece(rows, side)
+        if block == TO_OPPOSITE:
+            target, device = relay_in.at[rows, cols], (p.cross, p.mate)[side]
+        elif block == TO_CROSS:
+            target, device = ring_in.at[0, rows, cols], p.cross
+        else:
+            target, device = ring_in.at[1, rows, cols], p.mate
+        net.send(ring_index(block, rows, side), ring_out.at[block, rows, cols], target, device)
 
     for_sibling(TO_OPPOSITE, UPPER)
-    for_sibling(TO_CROSS, UPPER)
-    to_ring(TO_OPPOSITE, UPPER)
-    net.send(22, ring_out.at[TO_OPPOSITE, UPPER], relay_in.at[0], p.cross)
+    net.arrived(21, cots.at[OTHER, LOWER], p.opposite)
+    attend(OTHER, 0, LOWER)
+    for side in range(2):
+        to_ring(TO_OPPOSITE, UPPER, side)
+        ship(TO_OPPOSITE, UPPER, side)
     attend(OTHER, 1, LOWER)
     for_sibling(TO_OPPOSITE, LOWER)
-    for_sibling(TO_CROSS, LOWER)
-    to_ring(TO_OPPOSITE, LOWER)
-    net.send(23, ring_out.at[TO_OPPOSITE, LOWER], relay_in.at[1], p.mate)
+    for_sibling(TO_CROSS, UPPER)
+    for side in range(2):
+        to_ring(TO_OPPOSITE, LOWER, side)
+        ship(TO_OPPOSITE, LOWER, side)
     project(OWN, 1)
     attend(OWN, 1, UPPER)
     attend(OWN, 1, LOWER)
@@ -427,17 +487,22 @@
             my_up[:, pl.ds(at, 128)] = terms[RANK:, c0 + 384 : c0 + 512]
     my_up[:, 1536:UP] = jnp.broadcast_to(meta[OWN, 0:1, :], (RANK, 128)).astype(F32).astype(BF16)
     net.send(15, my_up, my_up, p.opposite)
-    to_ring(TO_CROSS, UPPER)
+    to_ring(TO_CROSS, UPPER, 0)
+    for_sibling(TO_MATE, UPPER)
     net.arrived(14, low_sib, p.sibling)
     low_chip[...] = (low_mine[...] + low_sib[...]).astype(BF16)
-    net.send(16, low_chip, low_in.at[0], p.mate)
-    net.send(17, low_chip, low_in.at[1], p.cross)
-    net.send(18, low_chip, low_in.at[2], p.opposite)
-    net.send(24, ring_out.at[TO_CROSS, UPPER], ring_in.at[0, UPPER], p.cross)
+    my_rank = pl.ds(pl.multiple_of(p.core * RANK, RANK), RANK)
+    for n, device in enumerate((p.mate, p.cross, p.opposite)):
+        net.send(16 + n, low_chip.at[:, my_rank], low_in.at[n], device)
+    ship(TO_CROSS, UPPER, 0)
+    to_ring(TO_MATE, UPPER, 1)
+    ship(TO_MATE, UPPER, 1)
+    for_sibling(TO_CROSS, LOWER)
     for_sibling(TO_MATE, LOWER)
-    for_sibling(TO_MATE, UPPER)
-    to_ring(TO_MATE, LOWER)
-    net.send(26, ring_out.at[TO_MATE, LOWER], ring_in.at[1, LOWER], p.mate)
+    to_ring(TO_CROSS, LOWER, 0)
+    ship(TO_CROSS, LOWER, 0)
+    to_ring(TO_MATE, LOWER, 1)
+    ship(TO_MATE, LOWER, 1)
 
     def terms_gather(base, ref, cuts):
         everything = slice(None)
@@ -449,16 +514,15 @@
 
         return [
             TorusGather(
-                net, base + 8 * n, p, n == 0, view,
-                slice(cuts[2 * n], cuts[2 * n + 2]),
+                net, base + 12 * n, p, n == 0, view,
                 slice(cuts[2 * n], cuts[2 * n + 1]),
                 slice(cuts[2 * n + 1], cuts[2 * n + 2]),
             )
             for n in range(2)
         ]
 
-    up_gather = terms_gather(72, up_terms, (0, 384, 768, 1152, UP))
-    down_gather = terms_gather(88, down_terms, (0, 640, 1152, 1792, DOWN))
+    up_gather = terms_gather(88, up_terms, (0, 384, 768, 1152, UP))
+    down_gather = terms_gather(112, down_terms, (0, 640, 1152, 1792, DOWN))
 
     def stage(gather, n):
         for one in gather:
@@ -466,56 +530,66 @@
 
     net.arrived(15, up_terms.at[1 - p.dp, p.y, p.z], p.opposite)
     stage(up_gather, 1)
-    for_sibling(TO_OWN, LOWER)
-    for_sibling(TO_OWN, UPPER)
-    to_ring(TO_MATE, UPPER)
-    net.arrived(22, relay_in.at[0], p.cross)
-    ring_out[TO_MATE, UPPER] = (
-        ring_out[TO_MATE, UPPER].astype(F32) + relay_in[0].astype(F32)
-    ).astype(BF16)
-    net.send(27, ring_out.at[TO_MATE, UPPER], ring_in.at[1, UPPER], p.mate)
-    stage(up_gather, 2)
 
     for n, device in enumerate((p.mate, p.cross, p.opposite)):
         net.arrived(16 + n, low_in.at[n], device)
+    for slot in (OWN, OTHER):
+        pair = low_chip[slot, my_rank].astype(F32) + low_in[0, slot].astype(F32)
+        far = low_in[1, 1 - slot].astype(F32) + low_in[2, 1 - slot].astype(F32)
+        low_grad[slot, my_rank] = (pair + far).astype(BF16)
+    swapped = low_grad.at[:, my_rank]
+    net.send(19, swapped, swapped, p.sibling)
+    stage(up_gather, 2)
+    to_ring(TO_MATE, UPPER, 0, True)
+    ship(TO_MATE, UPPER, 0)
+    other_rank = pl.ds(pl.multiple_of(away * RANK, RANK), RANK)
+    net.arrived(19, low_grad.at[:, other_rank], p.sibling)
     my_cols = pl.ds(pl.multiple_of(p.t * COLS, COLS), COLS)
-    low_grads = []
     for slot in (OWN, OTHER):
-        pair = low_chip[slot].astype(F32) + low_in[0, slot].astype(F32)
-        far = low_in[1, 1 - slot].astype(F32) + low_in[2, 1 - slot].astype(F32)
-        low_grads.append((pair + far).astype(BF16))
-        value = dot(low_grads[slot], xs[slot, :, my_cols], ((1,), (0,))).astype(BF16)
+        value = dot(low_grad[slot], xs[slot, :, my_cols], ((1,), (0,))).astype(BF16)
         my_down = down_terms.at[p.dp if slot == OWN else 1 - p.dp, p.y, p.z]
         my_down[:, 0:COLS] = value[:RANK]
         my_down[:, COLS:DOWN] = value[RANK:]
     stage(down_gather, 1)
-    to_ring(TO_CROSS, LOWER)
-    net.arrived(23, relay_in.at[1], p.mate)
-    ring_out[TO_CROSS, LOWER] = (
-        ring_out[TO_CROSS, LOWER].astype(F32) + relay_in[1].astype(F32)
-    ).astype(BF16)
-    net.send(25, ring_out.at[TO_CROSS, LOWER], ring_in.at[0, LOWER], p.cross)
     stage(up_gather, 3)
+    to_ring(TO_CROSS, UPPER, 1, True)
+    ship(TO_CROSS, UPPER, 1)
     stage(down_gather, 2)
-    for rows in (LOWER, UPPER):
-        for cols, value in both_cores(TO_OWN, rows):
-            kept[rows, cols] = value
-    kept[...] += dot(low_grads[OWN], down[OWN, :, my_cols], ((0,), (0,)))
+    to_ring(TO_MATE, LOWER, 0, True)
+    ship(TO_MATE, LOWER, 0)
+    to_ring(TO_CROSS, LOWER, 1, True)
+    ship(TO_CROSS, LOWER, 1)
     stage(down_gather, 3)
+    for_sibling(TO_OWN, UPPER)
+    for_sibling(TO_OWN, LOWER)
+
+    def keep(rows):
+        for side in range(2):
+            cols = piece(rows, side)
+            columns = pl.ds(pl.multiple_of(p.t * COLS + cols.start, 128), cols.stop - cols.start)
+            extra = dot(low_grad[OWN, :, rows], down[OWN, :, columns], ((0,), (0,)))
+            kept[rows, cols] = both_cores(TO_OWN, rows, side) + extra
+
+    keep(UPPER)
     stage(up_gather, 4)
+    keep(LOWER)
     stage(up_gather, 5)
     save_up = local(up_terms, up_out)
     stage(down_gather, 4)
+
+    def finish_rows(rows):
+        for side in range(2):
+            cols = piece(rows, side)
+            net.arrived(ring_index(TO_CROSS, rows, side), ring_in.at[0, rows, cols], p.cross)
+            net.arrived(ring_index(TO_MATE, rows, side), ring_in.at[1, rows, cols], p.mate)
+        grad_out[rows] = (
+            kept[rows] + ring_in[0, rows].astype(F32) + ring_in[1, rows].astype(F32)
+        ).astype(BF16)
+
+    finish_rows(UPPER)
     stage(down_gather, 5)
     save_down = local(down_terms, down_out)
-    for index, n, rows, device in (
-        (24, 0, UPPER, p.cross), (26, 1, LOWER, p.mate),
-        (27, 1, UPPER, p.mate), (25, 0, LOWER, p.cross),
-    ):
-        net.arrived(index, ring_in.at[n, rows], device)
-    grad_out[...] = (
-        kept[...] + ring_in[0].astype(F32) + ring_in[1].astype(F32)
-    ).astype(BF16)
+    finish_rows(LOWER)
     net.finish()
     save_up.wait()
     save_down.wait()
@@ -551,22 +625,25 @@
             bf16(2, TOKENS, 2 * GROUP),
             bf16(2, TOKENS, 512),
             pltpu.VMEM((2, 8, 128), jnp.int32),
-            f32(HALF, HD),
-            f32(HALF, HD),
+            f32(2, HALF, HD),
+            f32(2, HALF, HD),
             bf16(4, TOKENS, COLS),
             bf16(4, TOKENS, COLS),
             bf16(3, TOKENS, COLS),
-            bf16(2, HALF, COLS),
+            bf16(TOKENS, COLS),
             bf16(2, TOKENS, COLS),
             f32(TOKENS, COLS),
             f32(2, 2 * RANK, TOKENS),
             f32(2, 2 * RANK, TOKENS),
             bf16(2, 2 * RANK, TOKENS),
-            bf16(3, 2, 2 * RANK, TOKENS),
+            bf16(3, 2, RANK, TOKENS),
+            bf16(2, 2 * RANK, TOKENS),
             bf16(2, SIDE, SIDE, RANK, UP),
             bf16(2, SIDE, SIDE, RANK, DOWN),
-            pltpu.SemaphoreType.DMA((104,)),
-            pltpu.SemaphoreType.DMA((104,)),
+            f32(TOKENS, 2 * RANK),
+            f32(TOKENS, GROUP),
+            pltpu.SemaphoreType.DMA((152,)),
+            pltpu.SemaphoreType.DMA((152,)),
             pltpu.SemaphoreType.DMA((14,)),
         ],
         compiler_params=pltpu.CompilerParams(
@@ -575,46 +652,80 @@
     )(lengths, ids, *arrays)
 
 
-def table_kernel(grad_ref, up_ref, down_ref, grad_out, qa_out, qb_out, va_out, vb_out):
-    grad_out[...] = grad_ref[...]
+def table_kernel(
+    grad_ref, up_ref, down_ref, grad_out, qa_out, qb_out, va_out, vb_out,
+    grad, up, down, qa, qb, va, vb, in_sems, out_sems,
+):
+    width = 384
+    loads = [pltpu.make_async_copy(up_ref.at[s], up.at[s], in_sems.at[s]) for s in range(2)]
+    for n in range(2 * COLS // width):
+        cols = slice(n * width, (n + 1) * width)
+        loads.append(
+            pltpu.make_async_copy(down_ref.at[:, :, cols], down.at[:, :, cols], in_sems.at[2 + n])
+        )
+    loads.append(pltpu.make_async_copy(grad_ref, grad, in_sems.at[2 + 2 * COLS // width]))
+    for load in loads:
+        load.start()
+    stores = []
+
+    def store(src, dst):
+        copy = pltpu.make_async_copy(src, dst, out_sems.at[len(stores)])
+        copy.start()
+        stores.append(copy)
+
     rows = 16 * RANK
     at = lax.broadcasted_iota(jnp.int32, (rows, rows), 0)
     to = lax.broadcasted_iota(jnp.int32, (rows, rows), 1)
+    same = at % RANK == to % RANK
+    table = (to // RANK).astype(F32)
     owners = []
     for s in range(2):
-        chosen = up_ref[s, :, 1536:1537].astype(F32)
-        own = ((to // RANK).astype(F32) == chosen) & (at % RANK == to % RANK)
+        loads[s].wait()
+        chosen = up[s, :, 1536:1537].astype(F32)
+        own = (table == chosen) & same
         owners.append(own.astype(F32).T.astype(BF16))
 
     def total(first, second):
         return dot(owners[0], first, ((1,), (0,))) + dot(owners[1], second, ((1,), (0,)))
 
-    for c in range(0, COLS, 384):
-        cols = slice(c, c + 384)
-        qa_out[:, cols] = total(down_ref[0, :, cols], down_ref[1, :, cols])
-        cols = slice(COLS + c, COLS + c + 384)
-        va_out[:, c : c + 384] = total(down_ref[0, :, cols], down_ref[1, :, cols])
     for d in range(2):
-        for out, start, width in ((qb_out, 0, 512), (vb_out, 1024, 256)):
-            out[:, d * width : (d + 1) * width] = total(
-                up_ref[d, :, start : start + width],
-                up_ref[d, :, start + width : start + 2 * width],
+        for out, to_ref, start, size in ((qb, qb_out, 0, 512), (vb, vb_out, 1024, 256)):
+            cols = slice(d * size, (d + 1) * size)
+            out[:, cols] = total(
+                up[d, :, start : start + size], up[d, :, start + size : start + 2 * size]
             )
+            store(out.at[:, cols], to_ref.at[:, cols])
+    for n in range(2 * COLS // width):
+        loads[2 + n].wait()
+        out, to_ref, c = (qa, qa_out, 0) if n < COLS // width else (va, va_out, COLS)
+        cols = slice(n * width, (n + 1) * width)
+        here = slice(n * width - c, (n + 1) * width - c)
+        out[:, here] = total(down[0, :, cols], down[1, :, cols])
+        store(out.at[:, here], to_ref.at[:, here])
+    loads[-1].wait()
+    store(grad, grad_out)
+    for copy in stores:
+        copy.wait()
 
 
 def table_call(grad, up_terms, down_terms):
-    vmem = pl.BlockSpec(memory_space=pltpu.VMEM)
+    hbm = pl.BlockSpec(memory_space=pl.ANY)
     rows = 16 * RANK
-    table = lambda width: jax.ShapeDtypeStruct((rows, width), F32)
+    widths = (COLS, 1024, COLS, 512)
     return pl.pallas_call(
         table_kernel,
         name="tables",
-        out_shape=(
-            jax.ShapeDtypeStruct((TOKENS, COLS), BF16),
-            table(COLS), table(1024), table(COLS), table(512),
-        ),
-        in_specs=[vmem, vmem, vmem],
-        out_specs=(vmem, vmem, vmem, vmem, vmem),
+        out_shape=(jax.ShapeDtypeStruct((TOKENS, COLS), BF16),)
+        + tuple(jax.ShapeDtypeStruct((rows, width), F32) for width in widths),
+        in_specs=[hbm] * 3,
+        out_specs=(hbm,) * 5,
+        scratch_shapes=[
+            pltpu.VMEM((TOKENS, COLS), BF16),
+            pltpu.VMEM((2, rows, UP), BF16),
+            pltpu.VMEM((2, rows, DOWN), BF16),
+        ]
+        + [pltpu.VMEM((rows, width), F32) for width in widths]
+        + [pltpu.SemaphoreType.DMA((9,)), pltpu.SemaphoreType.DMA((11,))],
         compiler_params=pltpu.CompilerParams(vmem_limit_bytes=VMEM_BYTES),
     )(grad, up_terms.reshape(2, rows, UP), down_terms.reshape(2, rows, DOWN))
 

time: 132 us -> 126 us (0.955)
  Pallas kernels: 129 us -> 124 us
    pallas_call x1, Pallas kernels: 124 us -> 119 us  [block_call(): pl.pallas_call(block_kernel, name='attention_block', out_shape=(jax.Shape...]
where the time goes in v5:
time: 126 us
  Pallas kernels  124 us (98%)
  between operations  2.13 us (2%)
    pallas_call x1, Pallas kernels, block_call(): pl.pallas_call(block_kernel, name='attention_block', out_shape=(jax.Shape...  119 us
    pallas_call x1, Pallas kernels, table_call(): pl.pallas_call(table_kernel, name='tables', out_shape=(jax.ShapeDtypeStru...  5.2 us

profile of v5, /device:TPU:0, one launch (start us, length us, event | category | flops | bytes accessed | tf_op | source)
XLA Modules:
  0.0 126.0 jit_solution(6639586856077112708)
XLA Ops:
  1.9 118.7 %attention_block.1 = (bf16[512,1152]{1,0:T(8,128)(2,1)}, bf16[2,4,4,16,1664]{4,3,2,1,0:T(8,128)(2,1)}, bf16[2,4,4,16,2304]{4,3,2,1,0:T(8,128)(2,1)}) custom-call(s32[1]{0:T(128)S(6)} %copy.16.length_ref, s32[1]{0:T(128)S(6)} %copy.17.id_ref, bf16[512,1152]{1,0:T(8,128)(2,1)} %bitcast.11, bf16[512,1024]{1,0:T(8,128)(2,1)} %bitcast.12, ...), custom_call_target="tpu_custom_call" | custom-call | tf_op jit(solution)/shard_map/attention_block/pallas_call | solution.py:604
  120.6 5.2 %tables.1 = (bf16[512,1152]{1,0:T(8,128)(2,1)}, f32[256,1152]{1,0:T(8,128)}, f32[256,1024]{1,0:T(8,128)}, f32[256,1152]{1,0:T(8,128)}, f32[256,512]{1,0:T(8,128)}) custom-call(bf16[512,1152]{1,0:T(8,128)(2,1)} %get-tuple-element.13.grad_ref, bf16[2,256,1664]{2,1,0:T(8,128)(2,1)} %bitcast.10, bf16[2,256,2304]{2,1,0:T(8,128)(2,1)} %bitcast.9), custom_call_target="tpu_custom_call" | custom-call | tf_op jit(solution)/shard_map/tables/pallas_call | solution.py:715

commit v6 on v5

--- a/solution.py
+++ b/solution.py
@@ -17,8 +17,10 @@
 GROUP = 512
 COLS = 1152
 HALF = 256
-UP = 1536 + 128
+HEAD = 768
+UP = 2 * HEAD
 DOWN = 2 * COLS
+TAGGED = DOWN + 128
 
 soft_cap = 50.0
 adapter_scale = 2.0
@@ -155,7 +157,7 @@
 
 def block_kernel(
     length_ref, id_ref, x_ref, g_ref, wq_ref, wk_ref, wv_ref, qd_ref, vd_ref, qu_ref, vu_ref,
-    grad_out, up_out, down_out,
+    grad_out, owner_out, up_out, down_out,
     xs, ws, qds, vds, qus, vus, down, up, low, qkv, grads, cots, meta, dk_acc, dv_acc,
     sib_out, sib_in, ring_out, relay_in, ring_in, kept,
     low_mine, low_sib, low_chip, low_in, low_grad, up_terms, down_terms, low_acc, proj_acc,
@@ -430,79 +432,50 @@
         net.arrived(sib_index(block, rows, side), sib_in.at[block, rows, cols], p.sibling)
         return value + sib_in[block, rows, cols].astype(F32)
 
-    def ring_index(block, rows, side):
-        return 20 + 4 * block + 2 * (rows is UPPER) + side if block else (
-            32 + 2 * (rows is UPPER) + side
-        )
-
-    def to_ring(block, rows, side, relay=None):
+    def relayed(rows, side):
+        if rows is UPPER:
+            return ((32 + side, UPPER),)
+        return ((34 + side, slice(128, 256)), (176 + side, slice(0, 128)))
+
+    def to_ring(block, rows, side, relay=False):
         cols = piece(rows, side)
         value = both_cores(block, rows, side)
-        if relay is not None:
-            net.arrived(
-                ring_index(TO_OPPOSITE, rows, side), relay_in.at[rows, cols],
-                (p.cross, p.mate)[side],
-            )
+        if relay:
+            for index, part in relayed(rows, side):
+                net.arrived(index, relay_in.at[part, cols], (p.cross, p.mate)[side])
             value = value + relay_in[rows, cols].astype(F32)
         ring_out[block, rows, cols] = value.astype(BF16)
 
+    def ship_relayed(rows, side, n):
+        cols = piece(rows, side)
+        index, part = relayed(rows, side)[n]
+        net.send(
+            index, ring_out.at[TO_OPPOSITE, part, cols], relay_in.at[part, cols],
+            (p.cross, p.mate)[side],
+        )
+
+    def ring_index(block, rows, side):
+        return 20 + 4 * block + 2 * (rows is UPPER) + side
+
     def ship(block, rows, side):
         cols = piece(rows, side)
-        if block == TO_OPPOSITE:
-            target, device = relay_in.at[rows, cols], (p.cross, p.mate)[side]
-        elif block == TO_CROSS:
-            target, device = ring_in.at[0, rows, cols], p.cross
-        else:
-            target, device = ring_in.at[1, rows, cols], p.mate
-        net.send(ring_index(block, rows, side), ring_out.at[block, rows, cols], target, device)
-
-    for_sibling(TO_OPPOSITE, UPPER)
-    net.arrived(21, cots.at[OTHER, LOWER], p.opposite)
-    attend(OTHER, 0, LOWER)
-    for side in range(2):
-        to_ring(TO_OPPOSITE, UPPER, side)
-        ship(TO_OPPOSITE, UPPER, side)
-    attend(OTHER, 1, LOWER)
-    for_sibling(TO_OPPOSITE, LOWER)
-    for_sibling(TO_CROSS, UPPER)
-    for side in range(2):
-        to_ring(TO_OPPOSITE, LOWER, side)
-        ship(TO_OPPOSITE, LOWER, side)
-    project(OWN, 1)
-    attend(OWN, 1, UPPER)
-    attend(OWN, 1, LOWER)
-
-    for slot in (OWN, OTHER):
-        low_mine[slot] = adapter_scale * dot(up[slot], grads[slot], ((1,), (1,)))
-    net.send(14, low_mine, low_sib, p.sibling)
-    my_up = up_terms.at[p.dp, p.y, p.z]
-    for slot in (OWN, OTHER):
-        seq = p.dp if slot == OWN else 1 - p.dp
-        terms = (adapter_scale * dot(low[slot], grads[slot], ((0,), (0,)))).astype(BF16)
-        for g in range(2):
-            c0 = g * GROUP
-            at = pl.multiple_of(seq * 512 + g * 256, 256)
-            my_up[:, pl.ds(at, 256)] = terms[:RANK, c0 : c0 + 256]
-            at = pl.multiple_of(1024 + seq * 256 + g * 128, 128)
-            my_up[:, pl.ds(at, 128)] = terms[RANK:, c0 + 384 : c0 + 512]
-    my_up[:, 1536:UP] = jnp.broadcast_to(meta[OWN, 0:1, :], (RANK, 128)).astype(F32).astype(BF16)
-    net.send(15, my_up, my_up, p.opposite)
-    to_ring(TO_CROSS, UPPER, 0)
-    for_sibling(TO_MATE, UPPER)
-    net.arrived(14, low_sib, p.sibling)
-    low_chip[...] = (low_mine[...] + low_sib[...]).astype(BF16)
-    my_rank = pl.ds(pl.multiple_of(p.core * RANK, RANK), RANK)
-    for n, device in enumerate((p.mate, p.cross, p.opposite)):
-        net.send(16 + n, low_chip.at[:, my_rank], low_in.at[n], device)
-    ship(TO_CROSS, UPPER, 0)
-    to_ring(TO_MATE, UPPER, 1)
-    ship(TO_MATE, UPPER, 1)
-    for_sibling(TO_CROSS, LOWER)
-    for_sibling(TO_MATE, LOWER)
-    to_ring(TO_CROSS, LOWER, 0)
-    ship(TO_CROSS, LOWER, 0)
-    to_ring(TO_MATE, LOWER, 1)
-    ship(TO_MATE, LOWER, 1)
+        n, device = (0, p.cross) if block == TO_CROSS else (1, p.mate)
+        net.send(
+            ring_index(block, rows, side),
+            ring_out.at[block, rows, cols], ring_in.at[n, rows, cols], device,
+        )
+
+    def up_terms_of(g):
+        mine = up_terms.at[p.dp, p.y, p.z]
+        window = slice(g * GROUP, (g + 1) * GROUP)
+        for slot in (OWN, OTHER):
+            seq = p.dp if slot == OWN else 1 - p.dp
+            value = adapter_scale * dot(low[slot], grads[slot, :, window], ((0,), (0,)))
+            value = value.astype(BF16)
+            at = pl.multiple_of(g * HEAD + seq * 256, 256)
+            mine[:, pl.ds(at, 256)] = value[:RANK, :256]
+            at = pl.multiple_of(g * HEAD + 512 + seq * 128, 128)
+            mine[:, pl.ds(at, 128)] = value[RANK:, 384:]
 
     def terms_gather(base, ref, cuts):
         everything = slice(None)
@@ -522,46 +495,83 @@
         ]
 
     up_gather = terms_gather(88, up_terms, (0, 384, 768, 1152, UP))
-    down_gather = terms_gather(112, down_terms, (0, 640, 1152, 1792, DOWN))
+    down_gather = terms_gather(112, down_terms, (0, 640, 1280, 1920, TAGGED))
 
     def stage(gather, n):
         for one in gather:
             one.stage(n)
 
-    net.arrived(15, up_terms.at[1 - p.dp, p.y, p.z], p.opposite)
-    stage(up_gather, 1)
+    for_sibling(TO_OPPOSITE, UPPER)
+    for side in range(2):
+        to_ring(TO_OPPOSITE, UPPER, side)
+        ship_relayed(UPPER, side, 0)
+    net.arrived(21, cots.at[OTHER, LOWER], p.opposite)
+    attend(OTHER, 0, LOWER)
+    attend(OTHER, 1, LOWER)
+    up_terms_of(0)
+    for_sibling(TO_OPPOSITE, LOWER)
+    project(OWN, 1)
+    for side in range(2):
+        to_ring(TO_OPPOSITE, LOWER, side)
+        ship_relayed(LOWER, side, 0)
+    attend(OWN, 1, UPPER)
+    attend(OWN, 1, LOWER)
+
+    for slot in (OWN, OTHER):
+        low_mine[slot] = adapter_scale * dot(up[slot], grads[slot], ((1,), (1,)))
+    net.send(14, low_mine, low_sib, p.sibling)
+    up_terms_of(1)
+    net.arrived(14, low_sib, p.sibling)
+    low_chip[...] = (low_mine[...] + low_sib[...]).astype(BF16)
+    for n, device in enumerate((p.mate, p.cross, p.opposite)):
+        net.send(16 + n, low_chip, low_in.at[n], device)
+    my_up = up_terms.at[p.dp, p.y, p.z]
+    net.send(15, my_up, my_up, p.opposite)
+    for side in range(2):
+        ship_relayed(LOWER, side, 1)
+    for_sibling(TO_CROSS, UPPER)
+    for_sibling(TO_MATE, UPPER)
+    to_ring(TO_CROSS, UPPER, 0)
+    ship(TO_CROSS, UPPER, 0)
+    to_ring(TO_MATE, UPPER, 1)
+    ship(TO_MATE, UPPER, 1)
 
     for n, device in enumerate((p.mate, p.cross, p.opposite)):
         net.arrived(16 + n, low_in.at[n], device)
-    for slot in (OWN, OTHER):
-        pair = low_chip[slot, my_rank].astype(F32) + low_in[0, slot].astype(F32)
-        far = low_in[1, 1 - slot].astype(F32) + low_in[2, 1 - slot].astype(F32)
-        low_grad[slot, my_rank] = (pair + far).astype(BF16)
-    swapped = low_grad.at[:, my_rank]
-    net.send(19, swapped, swapped, p.sibling)
-    stage(up_gather, 2)
-    to_ring(TO_MATE, UPPER, 0, True)
-    ship(TO_MATE, UPPER, 0)
-    other_rank = pl.ds(pl.multiple_of(away * RANK, RANK), RANK)
-    net.arrived(19, low_grad.at[:, other_rank], p.sibling)
     my_cols = pl.ds(pl.multiple_of(p.t * COLS, COLS), COLS)
     for slot in (OWN, OTHER):
+        pair = low_chip[slot].astype(F32) + low_in[0, slot].astype(F32)
+        far = low_in[1, 1 - slot].astype(F32) + low_in[2, 1 - slot].astype(F32)
+        low_grad[slot] = (pair + far).astype(BF16)
         value = dot(low_grad[slot], xs[slot, :, my_cols], ((1,), (0,))).astype(BF16)
         my_down = down_terms.at[p.dp if slot == OWN else 1 - p.dp, p.y, p.z]
         my_down[:, 0:COLS] = value[:RANK]
         my_down[:, COLS:DOWN] = value[RANK:]
+        tag = jnp.broadcast_to(meta[slot, 0:1, :], (RANK, 128))
+        my_down[:, DOWN:TAGGED] = tag.astype(F32).astype(BF16)
     stage(down_gather, 1)
-    stage(up_gather, 3)
+    net.arrived(15, up_terms.at[1 - p.dp, p.y, p.z], p.opposite)
+    stage(up_gather, 1)
+    for_sibling(TO_CROSS, LOWER)
+    for_sibling(TO_MATE, LOWER)
+    stage(down_gather, 2)
+    to_ring(TO_CROSS, LOWER, 0)
+    ship(TO_CROSS, LOWER, 0)
+    to_ring(TO_MATE, LOWER, 1)
+    ship(TO_MATE, LOWER, 1)
+    stage(up_gather, 2)
+    to_ring(TO_MATE, UPPER, 0, True)
+    ship(TO_MATE, UPPER, 0)
     to_ring(TO_CROSS, UPPER, 1, True)
     ship(TO_CROSS, UPPER, 1)
-    stage(down_gather, 2)
+    stage(down_gather, 3)
     to_ring(TO_MATE, LOWER, 0, True)
     ship(TO_MATE, LOWER, 0)
     to_ring(TO_CROSS, LOWER, 1, True)
     ship(TO_CROSS, LOWER, 1)
-    stage(down_gather, 3)
     for_sibling(TO_OWN, UPPER)
     for_sibling(TO_OWN, LOWER)
+    stage(up_gather, 3)
 
     def keep(rows):
         for side in range(2):
@@ -571,11 +581,20 @@
             kept[rows, cols] = both_cores(TO_OWN, rows, side) + extra
 
     keep(UPPER)
+    stage(down_gather, 4)
+    keep(LOWER)
     stage(up_gather, 4)
-    keep(LOWER)
-    stage(up_gather, 5)
-    save_up = local(up_terms, up_out)
-    stage(down_gather, 4)
+    stage(down_gather, 5)
+    save = local(down_terms, down_out)
+
+    rows = 16 * RANK
+    at = lax.broadcasted_iota(jnp.int32, (rows, rows), 0)
+    to = lax.broadcasted_iota(jnp.int32, (rows, rows), 1)
+    for s in range(2):
+        chosen = down_terms[s, :, :, :, DOWN:TAGGED].reshape(rows, 128)[:, 0:1].astype(F32)
+        own = ((to // RANK).astype(F32) == chosen) & (at % RANK == to % RANK)
+        owner_out[s] = own.astype(F32).T.astype(BF16)
+
 
     def finish_rows(rows):
         for side in range(2):
@@ -587,12 +606,12 @@
         ).astype(BF16)
 
     finish_rows(UPPER)
-    stage(down_gather, 5)
-    save_down = local(down_terms, down_out)
+    stage(up_gather, 5)
+    save_up = local(up_terms, up_out)
     finish_rows(LOWER)
     net.finish()
     save_up.wait()
-    save_down.wait()
+    save.wait()
 
 
 def block_call(lengths, ids, *arrays):
@@ -606,11 +625,12 @@
         name="attention_block",
         out_shape=(
             jax.ShapeDtypeStruct((TOKENS, COLS), BF16),
+            jax.ShapeDtypeStruct((2, 16 * RANK, 16 * RANK), BF16),
             jax.ShapeDtypeStruct((2, SIDE, SIDE, RANK, UP), BF16),
-            jax.ShapeDtypeStruct((2, SIDE, SIDE, RANK, DOWN), BF16),
+            jax.ShapeDtypeStruct((2, SIDE, SIDE, RANK, TAGGED), BF16),
         ),
         in_specs=[smem, smem] + [hbm] * 9,
-        out_specs=(vmem, hbm, hbm),
+        out_specs=(vmem, vmem, hbm, hbm),
         scratch_shapes=[
             bf16(2, TOKENS, D),
             bf16(SIDE, COLS, 2 * GROUP),
@@ -636,15 +656,15 @@
             f32(2, 2 * RANK, TOKENS),
             f32(2, 2 * RANK, TOKENS),
             bf16(2, 2 * RANK, TOKENS),
-            bf16(3, 2, RANK, TOKENS),
+            bf16(3, 2, 2 * RANK, TOKENS),
             bf16(2, 2 * RANK, TOKENS),
             bf16(2, SIDE, SIDE, RANK, UP),
-            bf16(2, SIDE, SIDE, RANK, DOWN),
+            bf16(2, SIDE, SIDE, RANK, TAGGED),
             f32(TOKENS, 2 * RANK),
             f32(TOKENS, GROUP),
-            pltpu.SemaphoreType.DMA((152,)),
-            pltpu.SemaphoreType.DMA((152,)),
-            pltpu.SemaphoreType.DMA((14,)),
+            pltpu.SemaphoreType.DMA((178,)),
+            pltpu.SemaphoreType.DMA((178,)),
+            pltpu.SemaphoreType.DMA((16,)),
         ],
         compiler_params=pltpu.CompilerParams(
             collective_id=0, has_side_effects=True, vmem_limit_bytes=VMEM_BYTES
@@ -653,17 +673,19 @@
 
 
 def table_kernel(
-    grad_ref, up_ref, down_ref, grad_out, qa_out, qb_out, va_out, vb_out,
-    grad, up, down, qa, qb, va, vb, in_sems, out_sems,
+    grad_ref, owner_ref, up_ref, down_ref,
+    grad_out, qa_out, qb_out, va_out, vb_out,
+    grad, owners, up, down, qa, qb, va, vb, in_sems, out_sems,
 ):
     width = 384
-    loads = [pltpu.make_async_copy(up_ref.at[s], up.at[s], in_sems.at[s]) for s in range(2)]
+    pairs = [(owner_ref, owners), (up_ref, up)]
     for n in range(2 * COLS // width):
         cols = slice(n * width, (n + 1) * width)
-        loads.append(
-            pltpu.make_async_copy(down_ref.at[:, :, cols], down.at[:, :, cols], in_sems.at[2 + n])
-        )
-    loads.append(pltpu.make_async_copy(grad_ref, grad, in_sems.at[2 + 2 * COLS // width]))
+        pairs.append((down_ref.at[:, :, cols], down.at[:, :, cols]))
+    pairs.append((grad_ref, grad))
+    loads = [
+        pltpu.make_async_copy(src, dst, in_sems.at[n]) for n, (src, dst) in enumerate(pairs)
+    ]
     for load in loads:
         load.start()
     stores = []
@@ -673,28 +695,19 @@
         copy.start()
         stores.append(copy)
 
-    rows = 16 * RANK
-    at = lax.broadcasted_iota(jnp.int32, (rows, rows), 0)
-    to = lax.broadcasted_iota(jnp.int32, (rows, rows), 1)
-    same = at % RANK == to % RANK
-    table = (to // RANK).astype(F32)
-    owners = []
-    for s in range(2):
-        loads[s].wait()
-        chosen = up[s, :, 1536:1537].astype(F32)
-        own = (table == chosen) & same
-        owners.append(own.astype(F32).T.astype(BF16))
-
     def total(first, second):
         return dot(owners[0], first, ((1,), (0,))) + dot(owners[1], second, ((1,), (0,)))
 
-    for d in range(2):
-        for out, to_ref, start, size in ((qb, qb_out, 0, 512), (vb, vb_out, 1024, 256)):
-            cols = slice(d * size, (d + 1) * size)
-            out[:, cols] = total(
-                up[d, :, start : start + size], up[d, :, start + size : start + 2 * size]
-            )
-            store(out.at[:, cols], to_ref.at[:, cols])
+    for load in loads[:2]:
+        load.wait()
+    for out, to_ref, start, size in ((qb, qb_out, 0, 256), (vb, vb_out, 512, 128)):
+        for d in range(2):
+            for g in range(2):
+                at, first = (2 * d + g) * size, g * HEAD + start
+                out[:, at : at + size] = total(
+                    up[d, :, first : first + size], up[d, :, first + size : first + 2 * size]
+                )
+        store(out, to_ref)
     for n in range(2 * COLS // width):
         loads[2 + n].wait()
         out, to_ref, c = (qa, qa_out, 0) if n < COLS // width else (va, va_out, COLS)
@@ -708,7 +721,7 @@
         copy.wait()
 
 
-def table_call(grad, up_terms, down_terms):
+def table_call(grad, owners, *terms):
     hbm = pl.BlockSpec(memory_space=pl.ANY)
     rows = 16 * RANK
     widths = (COLS, 1024, COLS, 512)
@@ -717,28 +730,29 @@
         name="tables",
         out_shape=(jax.ShapeDtypeStruct((TOKENS, COLS), BF16),)
         + tuple(jax.ShapeDtypeStruct((rows, width), F32) for width in widths),
-        in_specs=[hbm] * 3,
+        in_specs=[hbm] * 4,
         out_specs=(hbm,) * 5,
         scratch_shapes=[
             pltpu.VMEM((TOKENS, COLS), BF16),
+            pltpu.VMEM((2, rows, rows), BF16),
             pltpu.VMEM((2, rows, UP), BF16),
             pltpu.VMEM((2, rows, DOWN), BF16),
         ]
         + [pltpu.VMEM((rows, width), F32) for width in widths]
-        + [pltpu.SemaphoreType.DMA((9,)), pltpu.SemaphoreType.DMA((11,))],
+        + [pltpu.SemaphoreType.DMA((10,)), pltpu.SemaphoreType.DMA((9,))],
         compiler_params=pltpu.CompilerParams(vmem_limit_bytes=VMEM_BYTES),
-    )(grad, up_terms.reshape(2, rows, UP), down_terms.reshape(2, rows, DOWN))
+    )(grad, owners, *(block.reshape(2, rows, -1) for block in terms))
 
 
 def shards(
     x_in, lengths, adapter_ids, attn_grad, w_query, w_key, w_value,
     query_down, query_up, value_down, value_up,
 ):
-    grad, up_terms, down_terms = block_call(
+    grad, owners, *terms = block_call(
         lengths, adapter_ids, x_in[0], attn_grad[0], w_query, w_key, w_value,
         query_down, value_down, query_up, value_up,
     )
-    grad, qa, qb, va, vb = table_call(grad, up_terms, down_terms)
+    grad, qa, qb, va, vb = table_call(grad, owners, *terms)
     tables = (table.reshape(ADAPTERS, RANK, -1) for table in (qa, qb, va, vb))
     return (grad[None], *tables)
 

time: 126 us -> 122 us (0.968)
  Pallas kernels: 124 us -> 120 us
    pallas_call x1, Pallas kernels: 119 us -> 114 us  [block_call(): pl.pallas_call(block_kernel, name='attention_block', out_shape=(jax.Shape...]
where the time goes in v6:
time: 122 us
  Pallas kernels  120 us (98%)
  between operations  2.13 us (2%)
    pallas_call x1, Pallas kernels, block_call(): pl.pallas_call(block_kernel, name='attention_block', out_shape=(jax.Shape...  114 us
    pallas_call x1, Pallas kernels, table_call(): pl.pallas_call(table_kernel, name='tables', out_shape=(jax.ShapeDtypeStru...  5.3 us

profile of v6, /device:TPU:0, one launch (start us, length us, event | category | flops | bytes accessed | tf_op | source)
XLA Modules:
  0.0 121.7 jit_solution(17234605021487582013)
XLA Ops:
  1.9 114.3 %attention_block.1 = (bf16[512,1152]{1,0:T(8,128)(2,1)}, bf16[2,256,256]{2,1,0:T(8,128)(2,1)}, bf16[2,4,4,16,1536]{4,3,2,1,0:T(8,128)(2,1)}, bf16[2,4,4,16,2432]{4,3,2,1,0:T(8,128)(2,1)}) custom-call(s32[1]{0:T(128)S(6)} %copy.16.length_ref, s32[1]{0:T(128)S(6)} %copy.17.id_ref, bf16[512,1152]{1,0:T(8,128)(2,1)} %bitcast.11, bf16[512,1024]{1,0:T(8,128)(2,1)} %bitcast.12, ...), custom_call_target="tpu_custom_call" | custom-call | tf_op jit(solution)/shard_map/attention_block/pallas_call | solution.py:623
  116.2 5.3 %tables.1 = (bf16[512,1152]{1,0:T(8,128)(2,1)}, f32[256,1152]{1,0:T(8,128)}, f32[256,1024]{1,0:T(8,128)}, f32[256,1152]{1,0:T(8,128)}, f32[256,512]{1,0:T(8,128)}) custom-call(bf16[512,1152]{1,0:T(8,128)(2,1)} %get-tuple-element.14.grad_ref, bf16[2,256,256]{2,1,0:T(8,128)(2,1)} %get-tuple-element.15.owner_ref, bf16[2,256,1536]{2,1,0:T(8,128)(2,1)} %bitcast.10, ...), custom_call_target="tpu_custom_call" | custom-call | tf_op jit(solution)/shard_map/tables/pallas_call | solution.py:728

commit v7 on v6

--- a/solution.py
+++ b/solution.py
@@ -508,7 +508,6 @@
     net.arrived(21, cots.at[OTHER, LOWER], p.opposite)
     attend(OTHER, 0, LOWER)
     attend(OTHER, 1, LOWER)
-    up_terms_of(0)
     for_sibling(TO_OPPOSITE, LOWER)
     project(OWN, 1)
     for side in range(2):
@@ -520,6 +519,7 @@
     for slot in (OWN, OTHER):
         low_mine[slot] = adapter_scale * dot(up[slot], grads[slot], ((1,), (1,)))
     net.send(14, low_mine, low_sib, p.sibling)
+    up_terms_of(0)
     up_terms_of(1)
     net.arrived(14, low_sib, p.sibling)
     low_chip[...] = (low_mine[...] + low_sib[...]).astype(BF16)
@@ -678,7 +678,9 @@
     grad, owners, up, down, qa, qb, va, vb, in_sems, out_sems,
 ):
     width = 384
-    pairs = [(owner_ref, owners), (up_ref, up)]
+    rows = 16 * RANK
+    pairs = [(owner_ref.at[s], owners.at[:, s * rows : (s + 1) * rows]) for s in range(2)]
+    pairs.append((up_ref, up))
     for n in range(2 * COLS // width):
         cols = slice(n * width, (n + 1) * width)
         pairs.append((down_ref.at[:, :, cols], down.at[:, :, cols]))
@@ -696,9 +698,10 @@
         stores.append(copy)
 
     def total(first, second):
-        return dot(owners[0], first, ((1,), (0,))) + dot(owners[1], second, ((1,), (0,)))
-
-    for load in loads[:2]:
+        one = dot(owners[:, :rows], first, ((1,), (0,)))
+        return one + dot(owners[:, rows:], second, ((1,), (0,)))
+
+    for load in loads[:3]:
         load.wait()
     for out, to_ref, start, size in ((qb, qb_out, 0, 256), (vb, vb_out, 512, 128)):
         for d in range(2):
@@ -709,11 +712,12 @@
                 )
         store(out, to_ref)
     for n in range(2 * COLS // width):
-        loads[2 + n].wait()
+        loads[3 + n].wait()
         out, to_ref, c = (qa, qa_out, 0) if n < COLS // width else (va, va_out, COLS)
         cols = slice(n * width, (n + 1) * width)
         here = slice(n * width - c, (n + 1) * width - c)
-        out[:, here] = total(down[0, :, cols], down[1, :, cols])
+        terms = down[:, :, cols].reshape(2 * rows, width)
+        out[:, here] = dot(owners[...], terms, ((1,), (0,)))
         store(out.at[:, here], to_ref.at[:, here])
     loads[-1].wait()
     store(grad, grad_out)
@@ -734,7 +738,7 @@
         out_specs=(hbm,) * 5,
         scratch_shapes=[
             pltpu.VMEM((TOKENS, COLS), BF16),
-            pltpu.VMEM((2, rows, rows), BF16),
+            pltpu.VMEM((rows, 2 * rows), BF16),
             pltpu.VMEM((2, rows, UP), BF16),
             pltpu.VMEM((2, rows, DOWN), BF16),
         ]

time: 122 us -> 122 us (level)
  no operation moved by 1% of the time
where the time goes in v7:
time: 122 us
  Pallas kernels  119 us (98%)
  between operations  2.13 us (2%)
    pallas_call x1, Pallas kernels, block_call(): pl.pallas_call(block_kernel, name='attention_block', out_shape=(jax.Shape...  114 us
    pallas_call x1, Pallas kernels, table_call(): pl.pallas_call(table_kernel, name='tables', out_shape=(jax.ShapeDtypeStru...  5.35 us

profile of v7, /device:TPU:0, one launch (start us, length us, event | category | flops | bytes accessed | tf_op | source)
XLA Modules:
  0.0 121.5 jit_solution(16668277054300780049)
XLA Ops:
  1.9 114.1 %attention_block.1 = (bf16[512,1152]{1,0:T(8,128)(2,1)}, bf16[2,256,256]{2,1,0:T(8,128)(2,1)}, bf16[2,4,4,16,1536]{4,3,2,1,0:T(8,128)(2,1)}, bf16[2,4,4,16,2432]{4,3,2,1,0:T(8,128)(2,1)}) custom-call(s32[1]{0:T(128)S(6)} %copy.16.length_ref, s32[1]{0:T(128)S(6)} %copy.17.id_ref, bf16[512,1152]{1,0:T(8,128)(2,1)} %bitcast.11, bf16[512,1024]{1,0:T(8,128)(2,1)} %bitcast.12, ...), custom_call_target="tpu_custom_call" | custom-call | tf_op jit(solution)/shard_map/attention_block/pallas_call | solution.py:623
  116.0 5.4 %tables.1 = (bf16[512,1152]{1,0:T(8,128)(2,1)}, f32[256,1152]{1,0:T(8,128)}, f32[256,1024]{1,0:T(8,128)}, f32[256,1152]{1,0:T(8,128)}, f32[256,512]{1,0:T(8,128)}) custom-call(bf16[512,1152]{1,0:T(8,128)(2,1)} %get-tuple-element.14.grad_ref, bf16[2,256,256]{2,1,0:T(8,128)(2,1)} %get-tuple-element.15.owner_ref, bf16[2,256,1536]{2,1,0:T(8,128)(2,1)} %bitcast.10, ...), custom_call_target="tpu_custom_call" | custom-call | tf_op jit(solution)/shard_map/tables/pallas_call | solution.py:732
